TPU v7x, 32 devices: a whole 2x2x4 slice. The times are simulated.
32 devices in a mesh: dp: 8 (over z, y), patch: 4 (over x, core).
Axes of the slice: x: 2, y: 2, z: 4, core: 2. Of those that a mesh axis runs over, the one named last changes fastest.
Arguments:
- description_vocabulary_ids: int32 [128, 32], P('dp'), may hold values from 0 to 15359
- description_place_indicator: int32 [128, 32], P('dp'), may hold values from 0 to 1, as said below
- paired_description_ids: int32 [128], P('dp'), may hold values from 0 to 127, each once
- picture_patch_encodings: bfloat16 [128, 128, 1408], P('dp', 'patch'), may hold values from -6 to 6
- incoming_adjoint_signal: bfloat16 [128, 64, 768], P('dp'), may hold values from -6 to 6
- trainable_probe_vectors: bfloat16 [32, 768], replicated, may hold values from -6 to 6
- vocabulary_vector_lookup: bfloat16 [15360, 768], P('patch'), may hold values from -6 to 6
- placement_vector_lookup: bfloat16 [32, 768], replicated, may hold values from -3 to 3
- lexicon_layernorm_stretch: float32 [768], replicated, may hold values from 0.5 to 1.5
- lexicon_layernorm_shift: float32 [768], replicated, may hold values from -1.5 to 1.5
- inward_attn_triple_proj: bfloat16 [768, 2304], replicated, may hold values from -0.21875 to 0.21875
- inward_attn_result_proj: bfloat16 [768, 768], replicated, may hold values from -0.625 to 0.625
- inward_layernorm_stretch: float32 [768], replicated, may hold values from 0.5 to 1.5
- inward_layernorm_shift: float32 [768], replicated, may hold values from -1.5 to 1.5
- between_attn_question_proj: bfloat16 [768, 768], replicated, may hold values from -0.21875 to 0.21875
- between_attn_lookup_proj: bfloat16 [1408, 768], P('patch'), may hold values from -0.15625 to 0.15625
- between_attn_content_proj: bfloat16 [1408, 768], P('patch'), may hold values from -0.15625 to 0.15625
- between_attn_result_proj: bfloat16 [768, 768], replicated, may hold values from -0.875 to 0.875
- between_layernorm_stretch: float32 [768], replicated, may hold values from 0.5 to 1.5
- between_layernorm_shift: float32 [768], replicated, may hold values from -1.5 to 1.5
- probe_mlp_first_proj: bfloat16 [768, 3072], replicated, may hold values from -0.21875 to 0.21875
- probe_mlp_second_proj: bfloat16 [3072, 768], replicated, may hold values from -0.15625 to 0.15625
- probe_mlp_layernorm_stretch: float32 [768], replicated, may hold values from 0.5 to 1.5
- probe_mlp_layernorm_shift: float32 [768], replicated, may hold values from -1.5 to 1.5
- sentence_mlp_first_proj: bfloat16 [768, 3072], replicated, may hold values from -0.21875 to 0.21875
- sentence_mlp_second_proj: bfloat16 [3072, 768], replicated, may hold values from -0.15625 to 0.15625
- sentence_mlp_layernorm_stretch: float32 [768], replicated, may hold values from 0.5 to 1.5
- sentence_mlp_layernorm_shift: float32 [768], replicated, may hold values from -1.5 to 1.5
- picture_alignment_proj: bfloat16 [768, 256], replicated, may hold values from -0.21875 to 0.21875
- sentence_alignment_proj: bfloat16 [768, 256], replicated, may hold values from -0.21875 to 0.21875
- sharpness_unbounded: float32 [], replicated, may hold values from 0.03 to 0.08
Outputs:
- hidden_out: bfloat16 [128, 64, 768], P('dp')
- loss: float32 [128], P('dp')
- features_grad: float32 [128, 128, 1408], P('dp', 'patch')
- query_tokens_grad: float32 [32, 768], P(None, 'dp')
- word_table_grad: float32 [15360, 768], P('patch')
- position_grad: float32 [32, 768], P(None, 'dp')
- emb_gain_grad: float32 [768], P('dp')
- emb_bias_grad: float32 [768], P('dp')
- qkv_weight_grad: float32 [768, 2304], P('dp')
- out_weight_grad: float32 [768, 768], P('dp')
- self_gain_grad: float32 [768], P('dp')
- self_bias_grad: float32 [768], P('dp')
- cross_query_grad: float32 [768, 768], P('dp')
- cross_key_grad: float32 [1408, 768], P('patch')
- cross_value_grad: float32 [1408, 768], P('patch')
- cross_out_grad: float32 [768, 768], P('dp')
- cross_gain_grad: float32 [768], P('dp')
- cross_bias_grad: float32 [768], P('dp')
- query_up_grad: float32 [768, 3072], P('dp')
- query_down_grad: float32 [3072, 768], P('dp')
- query_gain_grad: float32 [768], P('dp')
- query_bias_grad: float32 [768], P('dp')
- text_up_grad: float32 [768, 3072], P('dp')
- text_down_grad: float32 [3072, 768], P('dp')
- text_gain_grad: float32 [768], P('dp')
- text_bias_grad: float32 [768], P('dp')
- image_proj_grad: float32 [768, 256], P('dp')
- text_proj_grad: float32 [768, 256], P('dp')
- sharpness_derivative: float32 [], replicated
Inputs may be any that keep to these rules, and one draw needn't show every extreme that they name: `description_place_indicator`: each row is some ones followed by zeros, with 5 to 32 ones; some row has 32.
All inputs are finite; a program needn't handle non-finite values.
Results may differ from a plain program's by a relative error of at most 0.038.
Values may be sent and summed in bfloat16 or wider, within the bound.
No kernel may reach another device: no remote copies, remote signals or barrier semaphores. Data moves between devices by JAX's collectives and lax.ppermute only.
A program may use at most 256 MiB of HBM per device.

v0:
```python
import functools
import math

import jax
import jax.numpy as jnp
from jax import lax
from jax.experimental import pallas as pl
from jax.experimental.pallas import tpu as pltpu
from jax.sharding import Mesh, PartitionSpec as P

HEADS = 12
GROUP = 4
SLOTS = 128
CORES = 2
BF = jnp.bfloat16
F32 = jnp.float32
HIGHEST = lax.Precision.HIGHEST
VMEM_BYTES = 60 * 1024 * 1024
VMEM_SPARE = 10 * 1024 * 1024
SLAB = 32
DP, SHARE, PARTNER, CORE, MEMBER, OTHER = range(6)


def nn(a, b):
    return lax.dot_general(a, b, (((1,), (0,)), ((), ())), preferred_element_type=F32)


def nt(a, b):
    return lax.dot_general(a, b, (((1,), (1,)), ((), ())), preferred_element_type=F32)


def tn(a, b):
    return lax.dot_general(a, b, (((0,), (0,)), ((), ())), preferred_element_type=F32)


def exact(a, b, dims):
    return lax.dot_general(a, b, ((dims[0], dims[1]), ((), ())), precision=HIGHEST)


def normalise(values):
    centred = values - jnp.mean(values, axis=-1, keepdims=True)
    spread = jnp.mean(centred * centred, axis=-1, keepdims=True)
    scale = lax.rsqrt(spread + 1e-06)
    return centred * scale, scale


def slabs(rows):
    step = math.gcd(rows, SLAB)
    return [slice(r, r + step) for r in range(0, rows, step)]


def fold(values):
    return jnp.sum(values.reshape(-1, 8, values.shape[-1]), axis=0)


def norm_back(grad, normal, scale, gain):
    inner = grad * gain
    first = jnp.mean(inner, axis=-1, keepdims=True)
    second = jnp.mean(inner * normal, axis=-1, keepdims=True)
    return scale * (inner - first - normal * second), fold(grad * normal), fold(grad)


def norm_back_rows(grad_of, normal, scale, gain, put):
    gains = biases = None
    for at in slabs(normal.shape[0]):
        grad_in, part_gain, part_bias = norm_back(grad_of(at), normal[at], scale[at], gain[...])
        put(at, grad_in)
        gains = part_gain if gains is None else gains + part_gain
        biases = part_bias if biases is None else biases + part_bias
    return jnp.sum(gains, axis=0, keepdims=True), jnp.sum(biases, axis=0, keepdims=True)


def gelu_both(values):
    size = jnp.abs(values)
    t = 1.0 / (1.0 + (0.3275911 * math.sqrt(0.5)) * size)
    bell = jnp.exp(-0.5 * values * values)
    poly = t * (
        0.254829592
        + t * (-0.284496736 + t * (1.421413741 + t * (-1.453152027 + t * 1.061405429)))
    )
    tail = 0.5 * poly * bell
    cdf = jnp.where(values < 0, tail, 1.0 - tail)
    return values * cdf, cdf + values * bell * (1.0 / math.sqrt(2.0 * math.pi))


def order_weights(z_size, y_size, order):
    y_weights = [1 << k for k in range(y_size.bit_length() - 1)]
    z_weights = [y_size << k for k in range(z_size.bit_length() - 1)]
    return y_weights + z_weights if order == "y" else z_weights + y_weights


def relative_of(position, weights):
    last = len(weights) - 1
    return sum(w for k, w in enumerate(weights) if (position >> (last - k)) & 1)


def position_of(relative, weights):
    last = len(weights) - 1
    place = jnp.int32(0)
    for k, w in enumerate(weights):
        place = place + jnp.where((relative & w) != 0, 1 << (last - k), 0)
    return place


def choose_rows(info, share, weights, rows, size, width):
    blocks = []
    row = lax.broadcasted_iota(jnp.int32, (rows, width), 0)
    column = lax.broadcasted_iota(jnp.int32, (rows, width), 1)
    for position in range(1 << len(weights)):
        block = info[DP] ^ relative_of(position, weights)
        start = block * size + info[share] * rows
        blocks.append(jnp.where(column == row + start, 1.0, 0.0))
    return jnp.concatenate(blocks, axis=0).astype(BF)


def head_masks(lanes, head):
    lane = lax.broadcasted_iota(jnp.int32, (1, lanes), 1)
    return [(lane >= h * head) & (lane < (h + 1) * head) for h in range(lanes // head)]


def stack_heads(values, masks):
    zero = jnp.zeros_like(values)
    return jnp.concatenate([jnp.where(m, values, zero) for m in masks], axis=0)


def merge_heads(stacked, masks):
    rows = stacked.shape[0] // len(masks)
    total = None
    for h, m in enumerate(masks):
        piece = jnp.where(m, stacked[h * rows : (h + 1) * rows], 0.0)
        total = piece if total is None else total + piece
    return total


def softmax_into(out, scores, tile, scaling, closed=None):
    for r in range(0, scores.shape[0], tile):
        part = scores[r : r + tile] * scaling
        if closed is not None:
            part = part + closed
        top = jnp.max(part, axis=-1, keepdims=True)
        powers = jnp.exp(part - top)
        out[r : r + tile] = (powers / jnp.sum(powers, axis=-1, keepdims=True)).astype(BF)


def softmax_back(probs, grads, tile):
    parts = []
    for r in range(0, grads.shape[0], tile):
        p, dp = probs[r : r + tile].astype(F32), grads[r : r + tile]
        parts.append((p * (dp - jnp.sum(p * dp, axis=-1, keepdims=True))).astype(BF))
    return jnp.concatenate(parts, axis=0)


def whole(shape):
    zeros = (0,) * len(shape)
    return pl.BlockSpec(tuple(shape), lambda *_: zeros)


SCALARS = pl.BlockSpec(memory_space=pltpu.SMEM)


def call(kernel, ins, outs, *, grid=(), in_specs=None, out_specs=None, scratch=(), flops=0, name, after=(), weight=1):
    if in_specs is None:
        in_specs = [None] * len(ins)
    in_specs = [
        spec or (SCALARS if k == 0 else whole(v.shape))
        for k, (spec, v) in enumerate(zip(in_specs, ins))
    ]
    out_shape = [jax.ShapeDtypeStruct(shape, dtype) for shape, dtype in outs]
    if out_specs is None:
        out_specs = [None] * len(outs)
    out_specs = [spec or whole(o.shape) for spec, o in zip(out_specs, out_shape)]
    moved = sum(v.size * v.dtype.itemsize for v in list(ins) + out_shape)
    limit = VMEM_BYTES
    if not grid:
        held = sum(math.prod(v.shape) * jnp.dtype(v.dtype).itemsize for v in scratch)
        limit = min(VMEM_BYTES, moved + held + VMEM_SPARE)
    count = len(ins)

    def body(*refs):
        kernel(*refs[:count], *refs[count + len(after) :])

    return pl.pallas_call(
        body,
        grid=grid,
        in_specs=in_specs + [pl.BlockSpec(memory_space=pl.ANY)] * len(after),
        out_specs=out_specs,
        out_shape=out_shape,
        scratch_shapes=list(scratch),
        compiler_params=pltpu.CompilerParams(vmem_limit_bytes=limit),
        cost_estimate=pl.CostEstimate(
            flops=weight, bytes_accessed=1, transcendentals=0
        ),
        name=name,
    )(*ins, *after)


def words_kernel(info, ids, table, mine, give, total):
    step = pl.program_id(0)
    chunk = table.shape[0]

    @pl.when(step == 0)
    def _():
        total[...] = jnp.zeros_like(total)

    column = lax.broadcasted_iota(jnp.int32, (ids.shape[0], chunk), 1) + step * chunk
    hot = jnp.where(ids[...] == column, 1.0, 0.0).astype(BF)
    total[...] += nn(hot, table[...])

    @pl.when(step == pl.num_programs(0) - 1)
    def _():
        half = total.shape[0] // 2
        mine[...] = total[:half].astype(BF)
        give[...] = total[half:].astype(BF)


def look_up(info, ids, table, chunk=640):
    rows, width = table.shape
    count = ids.shape[0]
    return call(
        words_kernel,
        [info, ids, table],
        [((count // 2, width), BF)] * 2,
        grid=(rows // chunk,),
        in_specs=[None, None, pl.BlockSpec((chunk, width), lambda k: (k, 0))],
        scratch=[pltpu.VMEM((count, width), F32)],
        flops=2 * count * rows * width,
        name="words",
    )


def embed_slab(words, positions, at):
    slots, width = positions.shape
    total = words[0][at].astype(F32)
    for other in words[1:]:
        total = total + other[at].astype(F32)
    start = at.start % slots
    if start + total.shape[0] <= slots:
        return total + positions[start : start + total.shape[0]].astype(F32)
    return (total.reshape(-1, slots, width) + positions[...].astype(F32)[None]).reshape(-1, width)


def self_forward_kernel(
    x_size, weights, share_rows, info, positions, query_tokens, emb_gain, emb_bias, qkv,
    used, out_weight, gain, bias, cross_weight, *rest,
):
    words = rest[:x_size]
    (
        packed, probs, normal_q, normal_t, scale_q, scale_t, cross_q, keep, give, chosen_q, mixed,
        start_rows, query_rows, attended,
    ) = rest[x_size:]
    slots, width = positions.shape
    queries = query_tokens.shape[0]
    rows = queries + slots
    head = width // HEADS
    lanes = GROUP * head
    start_q = normalise(query_tokens[...].astype(F32))[0] * emb_gain[...] + emb_bias[...]
    count = words[0].shape[0]
    items = count // slots
    for at in slabs(count):
        normal, _ = normalise(embed_slab(words, positions, at))
        start_rows[at] = normal * emb_gain[...] + emb_bias[...]
    start_q_low, start_w_low = start_q.astype(BF), start_rows[...].astype(BF)
    both = jnp.concatenate([start_q_low, start_w_low], axis=0)
    for c in range(3):
        span = slice(c * width, (c + 1) * width)
        product = nn(both, qkv[:, span]).astype(BF)
        for i in range(items):
            packed[i * rows : i * rows + queries, span] = product[:queries]
            packed[i * rows + queries : (i + 1) * rows, span] = product[
                queries + i * slots : queries + (i + 1) * slots
            ]
    masks = head_masks(lanes, head)
    pair = 2 * rows
    row_item = lax.broadcasted_iota(jnp.int32, (pair, pair), 0) // rows
    column_item = lax.broadcasted_iota(jnp.int32, (pair, pair), 1) // rows
    for j in range(items // 2):
        closed = jnp.where((row_item == column_item) & (used[j : j + 1] > 0), 0.0, -1e30)
        at = slice(j * pair, (j + 1) * pair)
        for g in range(HEADS // GROUP):
            base = g * lanes
            q = stack_heads(packed[at, base : base + lanes], masks)
            k = packed[at, width + base : width + base + lanes]
            v = packed[at, 2 * width + base : 2 * width + base + lanes]
            p = probs.at[j * (HEADS // GROUP) + g]
            softmax_into(p, nt(q, k), pair, 1.0 / math.sqrt(head), closed)
            mixed[at, base : base + lanes] = merge_heads(nn(p[...], v), masks).astype(BF)
    attended[...] = nn(mixed[...], out_weight[...])
    for i in range(items):
        base = i * rows
        for at in slabs(queries):
            into = slice(i * queries + at.start, i * queries + at.stop)
            normal, scale = normalise(attended[base + at.start : base + at.stop] + start_q[at])
            normal_q[into] = normal
            scale_q[into] = scale
            query_rows[into] = (normal * gain[...] + bias[...]).astype(BF)
        for at in slabs(slots):
            into = slice(i * slots + at.start, i * slots + at.stop)
            start = base + queries + at.start
            normal, scale = normalise(
                attended[start : start + at.stop - at.start] + start_rows[into]
            )
            normal_t[into] = normal
            scale_t[into] = scale
    query_low = query_rows[...]
    cross_q[...] = nn(query_low, cross_weight[...]).astype(BF)
    size = width >> len(weights)
    for share, out in ((SHARE, keep), (PARTNER, give)):
        select = choose_rows(info, share, weights, share_rows, size, width)
        out[:, : items * slots] = nt(select, start_w_low).astype(BF)
        out[:, items * slots : items * (slots + rows)] = nt(select, mixed[...]).astype(BF)
        if share == SHARE:
            chosen_q[...] = nt(select, start_q_low).astype(BF)
        out[:, items * (slots + rows) :] = nt(select, query_low).astype(BF)


def self_forward(info, words, used, p, orders, share_rows):
    slots, width = p["positions"].shape
    queries = p["query_tokens"].shape[0]
    items = words[0].shape[0] // slots
    rows = queries + slots
    blocks = 1 << len(orders["y"])
    units = (items // 2) * (HEADS // GROUP)
    ins = [
        info, p["positions"], p["query_tokens"], p["emb_gain"], p["emb_bias"], p["qkv"], used,
        p["out"], p["self_gain"], p["self_bias"], p["cross_query"], *words,
    ]
    lhs = (blocks * share_rows, items * (slots + rows + queries))
    outs = [
        ((items * rows, 3 * width), BF),
        ((units, GROUP * 2 * rows, 2 * rows), BF),
        ((items * queries, width), F32),
        ((items * slots, width), F32),
        ((items * queries, 1), F32),
        ((items * slots, 1), F32),
        ((items * queries, width), BF),
        (lhs, BF),
        (lhs, BF),
        ((blocks * share_rows, queries), BF),
    ]
    return call(
        functools.partial(self_forward_kernel, len(words), orders["y"], share_rows),
        ins,
        outs,
        scratch=[
            pltpu.VMEM((items * rows, width), BF),
            pltpu.VMEM((items * slots, width), F32),
            pltpu.VMEM((items * queries, width), BF),
            pltpu.VMEM((items * rows, width), F32),
        ],
        flops=2 * items * rows * width * width * 6,
        name="self_forward",
    )


def fill_weights(places, shards, key_full, value_full):
    half = len(shards) // 2
    size = shards[0].shape[0]
    for k in range(half):
        at = pl.ds(pl.multiple_of(places[k] * size, 16), size)
        key_full[at, :] = shards[k][...]
        value_full[at, :] = shards[half + k][...]


def key_value_kernel(pieces, info, places, *rest):
    feats, shards = rest[:pieces], rest[pieces : 3 * pieces]
    keys, values, key_full, value_full = rest[3 * pieces :]
    fill_weights(places, shards, key_full, value_full)
    items, rows, width = feats[0].shape
    for k, piece in enumerate(feats):
        flat = piece[...].reshape(items * rows, width)
        at = slice(k * rows, (k + 1) * rows)
        keys[:, at] = nn(flat, key_full[...]).astype(BF).reshape(items, rows, -1)
        values[:, at] = nn(flat, value_full[...]).astype(BF).reshape(items, rows, -1)


def key_value(info, places, feats, shards, after):
    items, rows, deep = feats[0].shape
    width = shards[0].shape[1]
    pieces = len(feats)
    return call(
        functools.partial(key_value_kernel, pieces),
        [info, places, *feats, *shards],
        [((items, pieces * rows, width), BF)] * 2,
        in_specs=[SCALARS, SCALARS] + [None] * (3 * pieces),
        scratch=[pltpu.VMEM((deep, width), BF)] * 2,
        flops=4 * items * rows * pieces * deep * width,
        name="key_value",
        after=after,
    )


def cross_forward_kernel(
    weights, share_rows, info, cross_q, keys, values, normal_q, self_gain, self_bias,
    out_weight, probs, normal, scale, keep, give, mixed, added,
):
    items, _, width = keys.shape
    queries = cross_q.shape[0] // items
    head = width // HEADS
    lanes = GROUP * head
    masks = head_masks(lanes, head)
    groups = HEADS // GROUP
    for i in range(items):
        at = slice(i * queries, (i + 1) * queries)
        for g in range(groups):
            span = slice(g * lanes, (g + 1) * lanes)
            q = stack_heads(cross_q[at, span], masks)
            p = probs.at[i * groups + g]
            softmax_into(p, nt(q, keys[i, :, span]), 2 * queries, 1.0 / math.sqrt(head))
            mixed[at, span] = merge_heads(nn(p[...], values[i, :, span]), masks).astype(BF)
    added[...] = nn(mixed[...], out_weight[...])
    for at in slabs(added.shape[0]):
        n, s = normalise(added[at] + (normal_q[at] * self_gain[...] + self_bias[...]))
        normal[at] = n
        scale[at] = s
    for share, out in ((SHARE, keep), (PARTNER, give)):
        select = choose_rows(info, share, weights, share_rows, width >> len(weights), width)
        out[...] = nt(select, mixed[...]).astype(BF)


def cross_forward(info, cross_q, keys, values, normal_q, p, orders, share_rows):
    items, all_rows, width = keys.shape
    count = cross_q.shape[0]
    blocks = 1 << len(orders["z"])
    ins = [
        info, cross_q, keys, values, normal_q, p["self_gain"], p["self_bias"], p["cross_out"],
    ]
    outs = [
        ((items * HEADS // GROUP, GROUP * count // items, all_rows), BF),
        ((count, width), F32),
        ((count, 1), F32),
        ((blocks * share_rows, count), BF),
        ((blocks * share_rows, count), BF),
    ]
    return call(
        functools.partial(cross_forward_kernel, orders["y"], share_rows),
        ins,
        outs,
        scratch=[pltpu.VMEM((count, width), BF), pltpu.VMEM((count, width), F32)],
        flops=2 * count * width * width + 4 * count * all_rows * width,
        name="cross_forward",
    )


def ff_forward_kernel(
    weights, share_rows, averaged, info, normal_in, gain_in, bias_in, up, down, gain, bias, proj,
    slope, keep, give, normal, scale, final, raw, rows_low, total, inner, active_low,
):
    step = pl.program_id(0)
    blocks = 1 << len(weights)
    count, width = normal_in.shape
    chunk = up.shape[1]
    deep = 4 * share_rows
    size = 4 * width // blocks

    @pl.when(step == 0)
    def _():
        for at in slabs(count):
            rows = normal_in[at] * gain_in[...] + bias_in[...]
            rows_low[at] = rows.astype(BF)
            total[at] = rows
        for share, out in ((SHARE, keep), (PARTNER, give)):
            select = choose_rows(info, share, weights, share_rows, width // blocks, width)
            out[: blocks * share_rows] = nt(select, rows_low[...]).astype(BF)

    inner[...] = nn(rows_low[...], up[...])
    for at in slabs(count):
        for c in range(0, chunk, 256):
            value, slant = gelu_both(inner[at, c : c + 256])
            active_low[at, c : c + 256] = value.astype(BF)
            slope[at, c : c + 256] = slant.astype(BF)
    active = active_low[...]
    total[...] += nn(active, down[...])
    each = chunk // size
    row = lax.broadcasted_iota(jnp.int32, (deep, chunk), 0)
    column = lax.broadcasted_iota(jnp.int32, (deep, chunk), 1)
    for share, out in ((SHARE, keep), (PARTNER, give)):
        select = [
            jnp.where(column == row + (j * size + info[share] * deep), 1.0, 0.0)
            for j in range(each)
        ]
        picked = nt(jnp.concatenate(select, axis=0).astype(BF), active).astype(BF)
        for j in range(each):
            block = step * each + j
            place = position_of(block ^ info[DP], weights)
            at = pl.multiple_of(blocks * share_rows + place * deep, 16)
            out[pl.ds(at, deep), :] = picked[j * deep : (j + 1) * deep]

    @pl.when(step == pl.num_programs(0) - 1)
    def _():
        for at in slabs(count):
            n, s = normalise(total[at])
            normal[at] = n
            scale[at] = s
            final[at] = (n * gain[...] + bias[...]).astype(BF)
        low = final[...]
        items = raw.shape[0]
        if averaged:
            image = nn(low, proj[...]).reshape(items, count // items, -1)
            raw[...] = jnp.mean(image, axis=1)
        else:
            heads = jnp.concatenate(
                [low[i * (count // items) : i * (count // items) + 16] for i in range(items)], axis=0
            )
            text = nn(heads, proj[...]).reshape(items, 16, -1)
            raw[...] = text[:, 0]


def ff_forward(info, normal_in, gain_in, bias_in, names, p, weights, share_rows, items, averaged):
    up, down, gain, bias, proj = (p[k] for k in names)
    count, width = normal_in.shape
    inner = up.shape[1]
    chunk = width
    blocks = 1 << len(weights)
    lhs = (blocks * share_rows * 5, count)
    return call(
        functools.partial(ff_forward_kernel, weights, share_rows, averaged),
        [info, normal_in, gain_in, bias_in, up, down, gain, bias, proj],
        [
            ((count, inner), BF),
            (lhs, BF),
            (lhs, BF),
            ((count, width), F32),
            ((count, 1), F32),
            ((count, width), BF),
            ((items, proj.shape[1]), F32),
        ],
        grid=(inner // chunk,),
        in_specs=[None] * 4
        + [
            pl.BlockSpec((width, chunk), lambda k: (0, k)),
            pl.BlockSpec((chunk, width), lambda k: (k, 0)),
        ]
        + [None] * 3,
        out_specs=[pl.BlockSpec((count, chunk), lambda k: (0, k))] + [None] * 6,
        scratch=[
            pltpu.VMEM((count, width), BF),
            pltpu.VMEM((count, width), F32),
            pltpu.VMEM((count, chunk), F32),
            pltpu.VMEM((count, chunk), BF),
        ],
        flops=4 * count * width * inner,
        name="ff_forward",
    )


def ff_backward_kernel(
    averaged, info, incoming, extra, proj, normal, scale, gain, slope, up, down,
    rhs, grad_rows, vectors, added, outer, total,
):
    step = pl.program_id(0)
    count, width = normal.shape
    chunk = slope.shape[1]

    @pl.when(step == 0)
    def _():
        items = extra.shape[0] // 2
        each = count // items
        added[...] = nt(extra[...], proj[...])

        def grad_of(at):
            grad = incoming[at.start // each, at.start % each : at.start % each + SLAB].astype(F32)
            more = added[at.start // each : at.start // each + 1]
            if averaged:
                return grad + more
            row = lax.broadcasted_iota(jnp.int32, (SLAB, 1), 0) + at.start % each
            return grad + jnp.where(row == 0, more, 0.0)

        def put(at, grad_in):
            total[at] = grad_in
            outer[at] = grad_in.astype(BF)
            rhs[at, pl.num_programs(0) * chunk :] = grad_in.astype(BF)

        grads = norm_back_rows(grad_of, normal, scale, gain, put)
        vectors[...] = jnp.concatenate(grads, axis=0)

    inner = (nt(outer[...], down[...]) * slope[...].astype(F32)).astype(BF)
    rhs[:, pl.ds(pl.multiple_of(step * chunk, 128), chunk)] = inner
    total[...] += nt(inner, up[...])

    @pl.when(step == pl.num_programs(0) - 1)
    def _():
        grad_rows[...] = total[...]


def ff_backward(info, incoming, part_of, extra, state, names, p, averaged, after=()):
    up, down, gain, proj = (p[k] for k in names)
    slope, normal, scale = state
    count, width = normal.shape
    items = extra.shape[0] // 2
    inner = up.shape[1]
    chunk = width
    each = count // items
    gs = pltpu.PrefetchScalarGridSpec(
        num_scalar_prefetch=1,
        grid=(inner // chunk,),
        in_specs=[
            pl.BlockSpec((items, each, width), lambda k, info: (info[CORE], part_of, 0)),
            whole(extra.shape),
            whole(proj.shape),
            whole(normal.shape),
            whole(scale.shape),
            whole(gain.shape),
            pl.BlockSpec((count, chunk), lambda k, info: (0, k)),
            pl.BlockSpec((width, chunk), lambda k, info: (0, k)),
            pl.BlockSpec((chunk, width), lambda k, info: (k, 0)),
        ]
        + [pl.BlockSpec(memory_space=pl.ANY)] * len(after),
        out_specs=[whole((count, inner + width)), whole((count, width)), whole((2, width))],
        scratch_shapes=[
            pltpu.VMEM((2 * items, width), F32),
            pltpu.VMEM((count, width), BF),
            pltpu.VMEM((count, width), F32),
        ],
    )

    def body(*refs):
        ff_backward_kernel(averaged, *refs[:10], *refs[10 + len(after) :])

    return pl.pallas_call(
        body,
        grid_spec=gs,
        out_shape=[
            jax.ShapeDtypeStruct((count, inner + width), BF),
            jax.ShapeDtypeStruct((count, width), F32),
            jax.ShapeDtypeStruct((2, width), F32),
        ],
        compiler_params=pltpu.CompilerParams(vmem_limit_bytes=VMEM_BYTES),
        cost_estimate=pl.CostEstimate(
            flops=1, bytes_accessed=1, transcendentals=0
        ),
        name="ff_backward",
    )(info, incoming, extra, proj, normal, scale, gain, slope, up, down, *after)


def ff_weights_kernel(share_rows, blocks, info, lhs_a, lhs_b, rhs_a, rhs_b, keep, give, total):
    width = keep.shape[2]
    inner = rhs_a.shape[1] - width
    first = blocks * share_rows
    for c in range(inner // width):
        span = slice(c * width, (c + 1) * width)
        part = nn(lhs_a[:first], rhs_a[:, span]) + nn(lhs_b[:first], rhs_b[:, span])
        for b in range(blocks):
            total[b, c * share_rows : (c + 1) * share_rows] = part[
                b * share_rows : (b + 1) * share_rows
            ]
    deep = 4 * share_rows
    down = nn(lhs_a[first:], rhs_a[:, inner:]) + nn(lhs_b[first:], rhs_b[:, inner:])
    for b in range(blocks):
        out, at = (keep, b) if b < blocks // 2 else (give, b - blocks // 2)
        out[at, :deep] = total[b].astype(BF)
        out[at, deep:] = down[b * deep : (b + 1) * deep].astype(BF)


def ff_weights(info, lhs_a, lhs_b, rhs_a, rhs_b, share_rows, blocks, width, after):
    deep = 4 * share_rows
    out = ((blocks // 2, 2 * deep, width), BF)
    return call(
        functools.partial(ff_weights_kernel, share_rows, blocks),
        [info, lhs_a, lhs_b, rhs_a, rhs_b],
        [out, out],
        scratch=[pltpu.VMEM((blocks, deep, width), F32)],
        flops=4 * lhs_a.size * 4 * width,
        name="ff_weights",
        after=after,
    )


def log_sum(values, axis):
    top = jnp.max(values, axis=axis, keepdims=True)
    return top + jnp.log(jnp.sum(jnp.exp(values - top), axis=axis, keepdims=True))


def contrast_kernel(
    queries, slots, info, gathered, sharpness, loss, grad_image, grad_text, grad_sharp,
    all_loss, all_image, all_text,
):
    count = gathered.shape[0]
    emb = grad_image.shape[1]
    image_raw, text_raw = gathered[:, :emb], gathered[:, emb : 2 * emb]
    ids = gathered[:, 2 * emb :]
    pairs = ids[:, slots : slots + 1].astype(jnp.int32)
    pairs_row = ids.T[slots : slots + 1].astype(jnp.int32)
    image_scale = lax.rsqrt(jnp.sum(image_raw * image_raw, axis=1, keepdims=True) + 1e-06)
    text_scale = lax.rsqrt(jnp.sum(text_raw * text_raw, axis=1, keepdims=True) + 1e-06)
    image, text = image_raw * image_scale, text_raw * text_scale
    sharp = sharpness[...]
    factor = 1.0 / jnp.clip(sharp, 0.04, 0.5)
    inside = jnp.where((sharp >= 0.04) & (sharp <= 0.5), 1.0, 0.0)
    by_image = exact(image, text, ((1,), (1,))) * factor
    by_text = exact(text, image, ((1,), (1,))) * factor
    row, row_flat = log_sum(by_image, 1), log_sum(by_text, 0)
    column, column_flat = log_sum(by_text, 1), log_sum(by_image, 0)
    down = lax.broadcasted_iota(jnp.int32, (count, count), 0)
    across = lax.broadcasted_iota(jnp.int32, (count, count), 1)
    match = jnp.where(across == pairs, 1.0, 0.0)
    match_text = jnp.where(down == pairs_row, 1.0, 0.0)
    pull = 0.5 * (jnp.exp(by_image - row) + jnp.exp(by_image - column_flat)) - match
    pull_text = 0.5 * (jnp.exp(by_text - column) + jnp.exp(by_text - row_flat)) - match_text
    positive = jnp.sum(match * by_image, axis=1, keepdims=True)
    all_loss[...] = 0.5 * (row + column) - positive
    share = jnp.sum(jnp.sum(pull * by_image, axis=1, keepdims=True), axis=0, keepdims=True)
    grad_sharp[...] = -factor * inside * share
    toward_image = exact(pull, text, ((1,), (0,))) * factor
    toward_text = exact(pull_text, image, ((1,), (0,))) * factor
    all_image[...] = (
        image_scale
        * (toward_image - image * jnp.sum(image * toward_image, axis=1, keepdims=True))
        * (1.0 / queries)
    )
    all_text[...] = text_scale * (
        toward_text - text * jnp.sum(text * toward_text, axis=1, keepdims=True)
    )
    group = loss.shape[0]
    items = group // CORES
    base = info[DP] * group
    loss[...] = all_loss[pl.ds(pl.multiple_of(base, 8), group), :]
    mine = pl.ds(pl.multiple_of(base + info[CORE] * items, 8), items)
    theirs = pl.ds(pl.multiple_of(base + (1 - info[CORE]) * items, 8), items)
    grad_image[...] = jnp.concatenate([all_image[mine, :], all_image[theirs, :]], axis=0).astype(BF)
    grad_text[...] = jnp.concatenate([all_text[mine, :], all_text[theirs, :]], axis=0).astype(BF)


def contrast(info, gathered, sharpness, queries, slots, group, emb, after):
    count = gathered.shape[0]
    return call(
        functools.partial(contrast_kernel, queries, slots),
        [info, gathered, sharpness],
        [((group, 1), F32), ((group, emb), BF), ((group, emb), BF), ((1, 1), F32)],
        scratch=[
            pltpu.VMEM((count, 1), F32),
            pltpu.VMEM((count, emb), F32),
            pltpu.VMEM((count, emb), F32),
        ],
        flops=50 * count * count * emb,
        name="contrast",
        after=after,
    )


def cross_backward_kernel(
    info, grad_second, normal, scale, gain, out_weight, keys, values, probs, cross_q, cross_weight,
    rhs, grad_keys, grad_values, grad_query, vectors, grad_heads,
):
    items, _, width = keys.shape
    queries = cross_q.shape[0] // items
    head = width // HEADS
    lanes = GROUP * head
    scaling = 1.0 / math.sqrt(head)
    masks = head_masks(lanes, head)
    groups = HEADS // GROUP

    def put(at, grad_in):
        grad_query[at] = grad_in
        rhs[at, width:] = grad_in.astype(BF)

    grads = norm_back_rows(lambda at: grad_second[at], normal, scale, gain, put)
    vectors[...] = jnp.concatenate(grads, axis=0)
    grad_heads[...] = nt(rhs[:, width:], out_weight[...]).astype(BF)
    for i in range(items):
        at = slice(i * queries, (i + 1) * queries)
        for g in range(groups):
            span = slice(g * lanes, (g + 1) * lanes)
            dm = stack_heads(grad_heads[at, span], masks)
            q = stack_heads(cross_q[at, span], masks)
            p_low = probs[i * groups + g]
            ds = softmax_back(p_low, nt(dm, values[i, :, span]), 2 * queries)
            rhs[at, span] = (merge_heads(nn(ds, keys[i, :, span]), masks) * scaling).astype(BF)
            grad_keys[i, :, span] = (tn(ds, q) * scaling).astype(BF)
            grad_values[i, :, span] = tn(p_low, dm).astype(BF)
    grad_query[...] += nt(rhs[:, :width], cross_weight[...])


def cross_backward(info, grad_second, normal, scale, keys, values, probs, cross_q, p, after):
    items, all_rows, width = keys.shape
    count = cross_q.shape[0]
    return call(
        cross_backward_kernel,
        [
            info, grad_second, normal, scale, p["cross_gain"], p["cross_out"], keys, values, probs,
            cross_q, p["cross_query"],
        ],
        [
            ((count, 2 * width), BF),
            (keys.shape, BF),
            (keys.shape, BF),
            ((count, width), F32),
            ((2, width), F32),
        ],
        scratch=[pltpu.VMEM((count, width), BF)],
        flops=4 * count * width * width + 8 * count * all_rows * width,
        name="cross_backward",
        after=after,
    )


def features_kernel(pieces, info, places, grad_keys, grad_values, *rest):
    shards = rest[: 2 * pieces]
    mine, give, key_full, value_full = rest[2 * pieces :]
    fill_weights(places, shards, key_full, value_full)
    items, rows, deep = mine.shape
    for k, out in enumerate((mine, give)):
        at = slice(k * rows, (k + 1) * rows)
        grad = nt(grad_keys[:, at].reshape(items * rows, -1), key_full[...])
        grad = grad + nt(grad_values[:, at].reshape(items * rows, -1), value_full[...])
        out[...] = grad.reshape(items, rows, deep).astype(out.dtype)


def features_back(info, places, grad_keys, grad_values, shards, rows, after):
    items, _, width = grad_keys.shape
    pieces = len(shards) // 2
    deep = shards[0].shape[0] * pieces
    return call(
        functools.partial(features_kernel, pieces),
        [info, places, grad_keys, grad_values, *shards],
        [((items, rows, deep), F32), ((items, rows, deep), BF)],
        in_specs=[SCALARS, SCALARS] + [None] * (2 + len(shards)),
        scratch=[pltpu.VMEM((deep, width), BF)] * 2,
        flops=8 * items * rows * deep * width,
        name="features_back",
        after=after,
    )


def kv_weights_kernel(pieces, weights, cuts, info, grad_keys, grad_values, *rest):
    feats = rest[:pieces]
    keep, give, total, blocks = rest[pieces:]
    items, rows, deep = feats[0].shape
    width = grad_keys.shape[2]
    size = total.shape[0]
    row = lax.broadcasted_iota(jnp.int32, (size, deep), 0)
    column = lax.broadcasted_iota(jnp.int32, (size, deep), 1)
    for which, out in ((MEMBER, keep), (OTHER, give)):
        select = jnp.where(column == row + info[which] * size, 1.0, 0.0).astype(BF)
        for k, piece in enumerate(feats):
            at = slice(k * rows, (k + 1) * rows)
            picked = nt(select, piece[...].reshape(items * rows, deep)).astype(BF)
            part_k = nn(picked, grad_keys[:, at].reshape(items * rows, width))
            part_v = nn(picked, grad_values[:, at].reshape(items * rows, width))
            if k == 0:
                total[:, :width] = part_k
                total[:, width:] = part_v
            else:
                total[:, :width] += part_k
                total[:, width:] += part_v
        height, span = size // cuts[0], 2 * width // cuts[1]
        for a in range(cuts[0]):
            for b in range(cuts[1]):
                blocks[a * cuts[1] + b] = total[
                    a * height : (a + 1) * height, b * span : (b + 1) * span
                ].astype(BF)
        for position in range(cuts[0] * cuts[1]):
            if cuts[0] * cuts[1] == 1:
                out[0] = blocks[0]
            else:
                out[position] = blocks[info[DP] ^ relative_of(position, weights)]


def kv_weights(info, grad_keys, grad_values, feats, weights, size, cuts, after):
    width = grad_keys.shape[2]
    items, rows, deep = feats[0].shape
    blocks = (cuts[0] * cuts[1], size // cuts[0], 2 * width // cuts[1])
    return call(
        functools.partial(kv_weights_kernel, len(feats), weights, cuts),
        [info, grad_keys, grad_values, *feats],
        [(blocks, BF), (blocks, BF)],
        scratch=[pltpu.VMEM((size, 2 * width), F32), pltpu.VMEM(blocks, BF)],
        flops=4 * size * items * rows * len(feats) * (deep + 2 * width),
        name="kv_weights",
        after=after,
    )


def self_backward_kernel(
    x_size, info, grad_query, grad_text, normal_q, normal_t, scale_q, scale_t, gain, out_weight,
    packed, probs, positions, query_tokens, emb_gain, qkv, more, *rest,
):
    words = rest[:x_size]
    rhs, words_low, grad_mixed, attended, grad_packed, in_q, in_t = rest[x_size:]
    slots, width = positions.shape
    queries = query_tokens.shape[0]
    rows = queries + slots
    items = grad_text.shape[0] // slots
    count = items * slots
    head = width // HEADS
    lanes = GROUP * head
    scaling = 1.0 / math.sqrt(head)
    masks = head_masks(lanes, head)
    groups = HEADS // GROUP

    def put_rows(into, each, offset):
        def put(at, grad_in):
            into[at] = grad_in
            start = at.start // each * rows + offset + at.start % each
            attended[start : start + SLAB] = grad_in.astype(BF)

        return put

    gain_q, bias_q = norm_back_rows(
        lambda at: grad_query[at], normal_q, scale_q, gain, put_rows(in_q, queries, 0)
    )
    gain_t, bias_t = norm_back_rows(
        lambda at: grad_text[at], normal_t, scale_t, gain, put_rows(in_t, slots, queries)
    )
    half = items * rows // 2
    rhs[:half, 3 * width : 4 * width] = attended[:half]
    rhs[:half, 4 * width :] = attended[half:]
    grad_mixed[...] = nt(attended[...], out_weight[...]).astype(BF)
    pair = 2 * rows
    for j in range(items // 2):
        at = slice(j * pair, (j + 1) * pair)
        for g in range(groups):
            base = g * lanes
            q = stack_heads(packed[at, base : base + lanes], masks)
            k = packed[at, width + base : width + base + lanes]
            v = packed[at, 2 * width + base : 2 * width + base + lanes]
            dm = stack_heads(grad_mixed[at, base : base + lanes], masks)
            p_low = probs[j * groups + g]
            ds = softmax_back(p_low, nt(dm, v), pair)
            grad_packed[at, base : base + lanes] = (
                merge_heads(nn(ds, k), masks) * scaling
            ).astype(BF)
            grad_packed[at, width + base : width + base + lanes] = (tn(ds, q) * scaling).astype(BF)
            grad_packed[at, 2 * width + base : 2 * width + base + lanes] = tn(p_low, dm).astype(BF)
    total_q = None
    for i in range(items):
        piece = grad_packed[i * rows : i * rows + queries].astype(F32)
        total_q = piece if total_q is None else total_q + piece
        rhs[i * slots : (i + 1) * slots, : 3 * width] = grad_packed[
            i * rows + queries : (i + 1) * rows
        ]
    total_q = total_q.astype(BF)
    rhs[count : count + queries, : 3 * width] = total_q
    in_t[...] += nt(rhs[:count, : 3 * width], qkv[...])
    start_q = jnp.sum(in_q[...].reshape(items, queries, width), axis=0) + nt(total_q, qkv[...])
    normal_e, scale_e = normalise(query_tokens[...].astype(F32))
    grad_tokens, gain_e, bias_e = norm_back(start_q, normal_e, scale_e, emb_gain[...])
    gain_w, bias_w = gain_e, bias_e
    position_grad = None
    for at in slabs(count):
        normal_w, scale_w = normalise(embed_slab(words, positions, at))
        grad_words, part_gain, part_bias = norm_back(in_t[at], normal_w, scale_w, emb_gain[...])
        gain_w, bias_w = gain_w + part_gain, bias_w + part_bias
        words_low[at] = grad_words.astype(BF)
        position_grad = grad_words if position_grad is None else position_grad + grad_words
    rhs[count : count + queries, 3 * width : 4 * width] = grad_tokens.astype(BF)
    rhs[count : count + slots, 4 * width :] = position_grad.astype(BF)
    gain_w = jnp.sum(gain_w, axis=0, keepdims=True)
    bias_w = jnp.sum(bias_w, axis=0, keepdims=True)
    vectors = jnp.concatenate(
        [gain_w, bias_w, gain_q + gain_t, bias_q + bias_t]
        + [more[...], jnp.zeros((6, width), F32)],
        axis=0,
    )
    rhs[count + queries :, :width] = vectors.astype(BF)
    rhs[count + queries :, width:] = jnp.zeros((16, 4 * width), BF)


def self_backward(info, grad_query, grad_text, state, packed, probs, words, more, p, after):
    normal_q, normal_t, scale_q, scale_t = state
    slots, width = p["positions"].shape
    queries = p["query_tokens"].shape[0]
    items = words[0].shape[0] // slots
    rows = queries + slots
    count = items * slots
    ins = [
        info, grad_query, grad_text, normal_q, normal_t, scale_q, scale_t, p["self_gain"],
        p["out"], packed, probs, p["positions"], p["query_tokens"], p["emb_gain"], p["qkv"], more,
        *words,
    ]
    return call(
        functools.partial(self_backward_kernel, len(words)),
        ins,
        [((count + queries + 16, 5 * width), BF), ((count, width), BF)],
        scratch=[
            pltpu.VMEM((items * rows, width), BF),
            pltpu.VMEM((items * rows, width), BF),
            pltpu.VMEM((items * rows, 3 * width), BF),
            pltpu.VMEM((items * queries, width), F32),
            pltpu.VMEM((count, width), F32),
        ],
        flops=2 * items * rows * width * width * 7,
        name="self_backward",
        after=after,
    )


def spread_rows(grads, each, first_only):
    items, emb = grads.shape
    wide = jnp.broadcast_to(grads[:, None, :], (items, each, emb))
    if first_only:
        row = lax.broadcasted_iota(jnp.int32, (items, each, emb), 1)
        wide = jnp.where(row == 0, wide, 0.0)
    return wide.reshape(items * each, emb).astype(BF)


def mid_weights_kernel(
    weights, share_rows, info, query_a, query_b, mixed_a, mixed_b, rhs_a, rhs_b, final_a, final_b,
    text_a, text_b, grad_image, grad_text, out,
):
    count, width = final_a.shape
    items = grad_image.shape[0] // 2
    each = count // items
    blocks = 1 << len(weights)
    cross_q = nn(query_a[...], rhs_a[:, :width]) + nn(query_b[...], rhs_b[:, :width])
    cross_out = nn(mixed_a[...], rhs_a[:, width:]) + nn(mixed_b[...], rhs_b[:, width:])
    select = choose_rows(info, SHARE, weights, share_rows, width // blocks, width)
    image, text = grad_image[...].astype(F32), grad_text[...].astype(F32)
    proj_i = proj_t = None
    for k, (final, first) in enumerate(((final_a, text_a), (final_b, text_b))):
        at = slice(k * items, (k + 1) * items)
        part_i = nn(nt(select, final[...]).astype(BF), spread_rows(image[at], each, False))
        part_t = nn(nt(select, first[...]).astype(BF), spread_rows(text[at], each, True))
        proj_i = part_i if proj_i is None else proj_i + part_i
        proj_t = part_t if proj_t is None else proj_t + part_t
    top = jnp.concatenate([cross_q, proj_i], axis=1)
    low = jnp.concatenate([cross_out, proj_t], axis=1)
    for b in range(blocks):
        rows = slice(b * share_rows, (b + 1) * share_rows)
        out[b] = jnp.concatenate([top[rows], low[rows]], axis=0).astype(BF)


def mid_weights(
    info, query, mixed, rhs, final, text, grad_image, grad_text, weights, share_rows, after
):
    width = final[0].shape[1]
    emb = grad_image.shape[1]
    blocks = 1 << len(weights)
    out = ((blocks, 2 * share_rows, width + emb), BF)
    at = query[0].shape[1] - final[0].shape[0]
    lhs_spec = pl.BlockSpec(
        (query[0].shape[0], final[0].shape[0]), lambda *_: (0, at // final[0].shape[0])
    )
    return call(
        functools.partial(mid_weights_kernel, weights, share_rows),
        [info, *query, *mixed, *rhs, *final, *text, grad_image, grad_text],
        [out],
        grid=(1,),
        in_specs=[None, lhs_spec, lhs_spec] + [None] * 10,
        flops=4 * query[0].shape[0] * final[0].shape[0] * 4 * width,
        name="mid_weights",
        after=after,
        weight=10**11,
    )[0]


def last_weights_kernel(
    weights, share_rows, info, chosen_q, lhs_a, lhs_b, rhs_a, rhs_b, mid, keep, give
):
    width = rhs_a.shape[1] // 5
    blocks = 1 << len(weights)
    queries = chosen_q.shape[1]
    count = rhs_a.shape[0] - queries - 16
    select = choose_rows(info, SHARE, weights, share_rows, width // blocks, width)
    summed_q = (
        rhs_a[count : count + queries, : 3 * width].astype(F32)
        + rhs_b[count : count + queries, : 3 * width].astype(F32)
    ).astype(BF)
    qkv = nn(chosen_q[...], summed_q)
    out_grad = vector_grad = None
    for lhs, rhs in ((lhs_a, rhs_a), (lhs_b, rhs_b)):
        qkv = qkv + nn(lhs[:, :count], rhs[:count, : 3 * width])
        part = nn(lhs[:, count : 2 * count], rhs[:count, 3 * width : 4 * width])
        part = part + nn(lhs[:, 2 * count : 3 * count], rhs[:count, 4 * width :])
        out_grad = part if out_grad is None else out_grad + part
        rows = jnp.concatenate(
            [
                rhs[count : count + queries, 3 * width : 4 * width],
                rhs[count : count + queries, 4 * width :],
                rhs[count + queries :, :width],
                jnp.zeros((128 - 2 * queries - 16, width), BF),
            ],
            axis=0,
        )
        part = nt(select, rows)
        vector_grad = part if vector_grad is None else vector_grad + part
    split = 2 * width
    top = jnp.concatenate([qkv[:, :split], vector_grad], axis=1)
    low = jnp.concatenate([qkv[:, split:], out_grad, jnp.zeros_like(vector_grad)], axis=1)
    base = mid.shape[2]
    for b in range(blocks):
        out, at = (keep, b) if b < blocks // 2 else (give, b - blocks // 2)
        rows = slice(b * share_rows, (b + 1) * share_rows)
        out[at, :, :base] = mid[b]
        out[at, :, base:] = jnp.concatenate([top[rows], low[rows]], axis=0).astype(BF)


def last_weights(info, chosen_q, lhs, rhs, mid, weights, share_rows, after):
    width = rhs[0].shape[1] // 5
    blocks = 1 << len(weights)
    out = ((blocks // 2, 2 * share_rows, mid.shape[2] + 2 * width + 128), BF)
    return call(
        functools.partial(last_weights_kernel, weights, share_rows),
        [info, chosen_q, *lhs, *rhs, mid],
        [out, out],
        flops=4 * chosen_q.shape[0] * 256 * 6 * width,
        name="last_weights",
        after=after,
    )


def ff_assemble_kernel(pieces, share_rows, info, places, *rest):
    parts = rest[:pieces]
    outs = rest[pieces:]
    width = parts[0].shape[1]
    deep = 4 * share_rows
    for k, piece in enumerate(parts):
        for f in range(2):
            up, down = outs[2 * f : 2 * f + 2]
            base = f * 2 * deep
            grad = piece[base : base + deep].astype(F32)
            at = pl.ds(pl.multiple_of(places[k] * share_rows, 8), share_rows)
            for c in range(4):
                up[at, c * width : (c + 1) * width] = grad[c * share_rows : (c + 1) * share_rows]
            at = pl.ds(pl.multiple_of(places[k] * deep, 8), deep)
            down[at, :] = piece[base + deep : base + 2 * deep].astype(F32)


def ff_assemble(info, places, parts, share_rows):
    width = parts[0].shape[1]
    rows = share_rows * len(parts)
    shapes = [((rows, 4 * width), F32), ((4 * rows, width), F32)] * 2
    return call(
        functools.partial(ff_assemble_kernel, len(parts), share_rows),
        [info, places, *parts],
        shapes,
        in_specs=[SCALARS, SCALARS] + [None] * len(parts),
        name="ff_assemble",
    )


def tail_assemble_kernel(pieces, share_rows, queries, info, places, *rest):
    parts = rest[:pieces]
    qkv, out, cross_q, cross_out, image, text, tokens, slots, vectors, spread = rest[pieces:]
    width = out.shape[1]
    emb = image.shape[1]
    spread[...] = jnp.zeros_like(spread)
    for k, piece in enumerate(parts):
        at = pl.ds(pl.multiple_of(places[k] * share_rows, 8), share_rows)
        grad = piece[...].astype(F32)
        top, low = grad[:share_rows], grad[share_rows:]
        cross_q[at, :] = top[:, :width]
        image[at, :] = top[:, width : width + emb]
        cross_out[at, :] = low[:, :width]
        text[at, :] = low[:, width : width + emb]
        base = width + emb
        qkv[at, : 2 * width] = top[:, base : base + 2 * width]
        spread[at, :] = top[:, base + 2 * width :]
        qkv[at, 2 * width :] = low[:, base : base + width]
        out[at, :] = low[:, base + width : base + 2 * width]
    flipped = spread[...].T
    rows = out.shape[0]
    tokens[...] = flipped[:queries, :rows]
    slots[...] = flipped[queries : 2 * queries, :rows]
    vectors[...] = flipped[2 * queries : 2 * queries + 16, :rows]


def tail_assemble(info, places, parts, share_rows, width, emb, queries):
    rows = share_rows * len(parts)
    shapes = [
        ((rows, 3 * width), F32),
        ((rows, width), F32),
        ((rows, width), F32),
        ((rows, width), F32),
        ((rows, emb), F32),
        ((rows, emb), F32),
        ((queries, rows), F32),
        ((queries, rows), F32),
        ((16, rows), F32),
    ]
    return call(
        functools.partial(tail_assemble_kernel, len(parts), share_rows, queries),
        [info, places, *parts],
        shapes,
        in_specs=[SCALARS, SCALARS] + [None] * len(parts),
        scratch=[pltpu.VMEM((128, 128), F32)],
        name="tail_assemble",
    )


def kv_assemble_kernel(count, weights, cuts, info, *rest):
    parts = rest[:count]
    key, value, blocks = rest[count:]
    at = 0
    for piece in parts:
        for b in range(piece.shape[0]):
            blocks[info[DP] ^ relative_of(at, weights)] = piece[b].astype(F32)
            at += 1
    height, span = blocks.shape[1:]
    width = key.shape[1]
    for a in range(cuts[0]):
        for b in range(cuts[1]):
            out = key if b * span < width else value
            base = b * span % width
            out[a * height : (a + 1) * height, base : base + span] = blocks[a * cuts[1] + b]


def kv_assemble(info, parts, weights, cuts, width):
    height, span = parts[0].shape[1:]
    shape = ((height * cuts[0], width), F32)
    return call(
        functools.partial(kv_assemble_kernel, len(parts), weights, cuts),
        [info, *parts],
        [shape, shape],
        scratch=[pltpu.VMEM((cuts[0] * cuts[1], height, span), F32)],
        name="kv_assemble",
    )


def features_assemble_kernel(info, mine, theirs, out):
    @pl.when(pl.program_id(0) == info[CORE])
    def _():
        out[...] = mine[...]

    @pl.when(pl.program_id(0) != info[CORE])
    def _():
        out[...] = theirs[...].astype(F32)


def features_assemble(info, mine, theirs):
    items, rows, deep = mine.shape
    return call(
        features_assemble_kernel,
        [info, mine, theirs],
        [((CORES * items, rows, deep), F32)],
        grid=(CORES,),
        out_specs=[pl.BlockSpec((items, rows, deep), lambda k: (k, 0, 0))],
        name="features_assemble",
    )[0]


def hidden_assemble_kernel(info, query_a, text_a, query_b, text_b, out):
    items = out.shape[0]
    queries = query_a.shape[0] // items
    mine = pl.program_id(0) == info[CORE]

    def put(query, text):
        out[:, :queries] = query[...].reshape(items, queries, -1)
        out[:, queries:] = text[...].reshape(items, -1, out.shape[2])

    @pl.when(mine)
    def _():
        put(query_a, text_a)

    @pl.when(jnp.logical_not(mine))
    def _():
        put(query_b, text_b)


def hidden_assemble(info, query_a, text_a, query_b, text_b, items):
    width = query_a.shape[1]
    rows = (query_a.shape[0] + text_a.shape[0]) // items
    return call(
        hidden_assemble_kernel,
        [info, query_a, text_a, query_b, text_b],
        [((CORES * items, rows, width), BF)],
        grid=(CORES,),
        out_specs=[pl.BlockSpec((items, rows, width), lambda k: (k, 0, 0))],
        name="hidden_assemble",
    )[0]


def slots_kernel(
    table_rows, patch_size, info, tokens, slot_of, rows_of, most
):
    groups, count = tokens.shape
    here_from = info[MEMBER] * table_rows
    all_rows = tokens[...]
    flipped = all_rows.T
    place = lax.broadcasted_iota(jnp.int32, (groups, count), 1)
    step = math.gcd(count, 64)
    down = lax.broadcasted_iota(jnp.int32, (step, count), 0)

    def over_slabs(d, make, combine):
        total = None
        for r in range(0, count, step):
            part = make(d, r)
            total = part if total is None else combine(total, part)
        return total

    def first_of(d, r):
        same = flipped[r : r + step, d : d + 1] == all_rows[d : d + 1]
        return jnp.min(jnp.where(same, down + r, count), axis=0, keepdims=True)

    first = jnp.concatenate(
        [over_slabs(d, first_of, jnp.minimum) for d in range(groups)], axis=0
    )
    here = (all_rows >= here_from) & (all_rows < here_from + table_rows)
    lead = first == place
    leads = jnp.where(lead & here, 1, 0).T

    def ahead_of(d, r):
        ahead = jnp.where(down + r < first[d : d + 1], leads[r : r + step, d : d + 1], 0)
        return jnp.sum(ahead, axis=0, keepdims=True)

    slot = jnp.concatenate([over_slabs(d, ahead_of, jnp.add) for d in range(groups)], axis=0)
    slot = jnp.where(here, slot, -1)
    slot_of[...] = slot
    slot_down = slot.T
    slot_iota = lax.broadcasted_iota(jnp.int32, (step, SLOTS), 1)

    def row_of(d, r):
        hit = slot_down[r : r + step, d : d + 1] == slot_iota
        local = flipped[r : r + step, d : d + 1] - here_from
        return jnp.max(jnp.where(hit, local, -1), axis=0, keepdims=True)

    for d in range(groups):
        rows_of[:, d * SLOTS : (d + 1) * SLOTS] = over_slabs(d, row_of, jnp.maximum)
    top = jnp.zeros((1, 1), jnp.int32)
    for q in range(patch_size):
        within = lead & (all_rows >= q * table_rows) & (all_rows < (q + 1) * table_rows)
        each = jnp.sum(jnp.where(within, 1, 0), axis=1, keepdims=True)
        top = jnp.maximum(top, jnp.max(each, axis=0, keepdims=True))
    most[...] = top


def slots_of(info, tokens, table_rows, patch_size, after):
    groups, count = tokens.shape
    return call(
        functools.partial(slots_kernel, table_rows, patch_size),
        [info, tokens],
        [
            ((groups, count), jnp.int32),
            ((1, groups * SLOTS), jnp.int32),
            ((1, 1), jnp.int32),
        ],
        flops=groups * count * count * 8,
        name="slots",
        after=after,
        weight=10**11,
    )


def collect_kernel(info, slot_of, mine, theirs, out):
    count = mine.shape[0]
    slot = lax.broadcasted_iota(jnp.int32, (SLOTS, count), 0)
    total = None
    for rows, core in ((mine, info[CORE]), (theirs, 1 - info[CORE])):
        at = pl.ds(pl.multiple_of(core * count, 128), count)
        hot = jnp.where(slot_of[pl.ds(info[DP], 1), at] == slot, 1.0, 0.0).astype(BF)
        part = nn(hot, rows[...])
        total = part if total is None else total + part
    out[...] = total.astype(BF)


def collect(info, slot_of, mine, theirs, after):
    return call(
        collect_kernel,
        [info, slot_of, mine, theirs],
        [((SLOTS, mine.shape[1]), BF)],
        flops=4 * SLOTS * mine.size,
        name="collect",
        after=after,
    )[0]


def table_kernel(z_size, y_size, info, rows_of, own, *rest):
    rising, falling = rest[: z_size - 1], rest[z_size - 1 : 2 * (z_size - 1)]
    out, ordered = rest[2 * (z_size - 1) :]
    chunk = out.shape[0]

    @pl.when(pl.program_id(0) == 0)
    def _():
        z, y = info[DP] // y_size, info[DP] % y_size

        def put(piece, at_z):
            for j in range(y_size):
                at = pl.multiple_of((at_z * y_size + (y ^ j)) * SLOTS, SLOTS)
                ordered[pl.ds(at, SLOTS), :] = piece[j * SLOTS : (j + 1) * SLOTS]

        put(own, z)
        for k in range(1, z_size):

            @pl.when(z - k >= 0)
            def _():
                put(rising[k - 1], z - k)

            @pl.when(z + k < z_size)
            def _():
                put(falling[k - 1], z + k)

    row = lax.broadcasted_iota(jnp.int32, (chunk, rows_of.shape[1]), 0)
    row = row + pl.program_id(0) * chunk
    hot = jnp.where(row == rows_of[...], 1.0, 0.0).astype(BF)
    out[...] = nn(hot, ordered[...])


def table_back(info, rows_of, own, rising, falling, z_size, y_size, table_rows, chunk=640):
    width = own.shape[1]
    count = rows_of.shape[1]
    return call(
        functools.partial(table_kernel, z_size, y_size),
        [info, rows_of, own, *rising, *falling],
        [((table_rows, width), F32)],
        grid=(table_rows // chunk,),
        out_specs=[pl.BlockSpec((chunk, width), lambda k: (k, 0))],
        scratch=[pltpu.VMEM((count, width), BF)],
        flops=2 * table_rows * count * width,
        name="table",
    )[0]


def stage_kernel(info, *refs):
    half = len(refs) // 2
    for given, out in zip(refs[:half], refs[half:]):
        out[...] = given[...]


def stage(info, values, after):
    return call(
        stage_kernel, [info, *values], [(v.shape, v.dtype) for v in values], name="stage",
        after=after,
    )


def swap_core(values):
    return lax.ppermute(values, "core", [(0, 1), (1, 0)])


def from_x(values, size, step):
    return lax.ppermute(values, "x", [(s, (s - step) % size) for s in range(size)])


def part(values, index, size, axis):
    return lax.dynamic_slice_in_dim(values, index * size, size, axis)


def exchange(values, axis, size, bit):
    return lax.ppermute(values, axis, [(s, s ^ bit) for s in range(size)])


def gather_doubling(values, axis, size):
    place = lax.axis_index(axis)
    bit = 1
    while bit < size:
        other = exchange(values, axis, size, bit)
        low = (place & bit) == 0
        values = jnp.concatenate(
            [jnp.where(low, values, other), jnp.where(low, other, values)], axis=0
        )
        bit *= 2
    return values


def gather_relative(values, axis, size):
    bit = 1
    while bit < size:
        values = jnp.concatenate([values, exchange(values, axis, size, bit)], axis=0)
        bit *= 2
    return values


def pass_on(values, axis, size):
    up = [(s, s + 1) for s in range(size - 1)]
    down = [(s + 1, s) for s in range(size - 1)]
    rising, falling = [values], [values]
    for _ in range(1, size):
        rising.append(lax.ppermute(rising[-1], axis, up))
        falling.append(lax.ppermute(falling[-1], axis, down))
    return rising[1:], falling[1:]


def gather_patch(values, x_size):
    own = [values] + [from_x(values, x_size, k) for k in range(1, x_size)]
    return own + [swap_core(v) for v in own]


def patch_places(x_size):
    xi, ci = lax.axis_index("x"), lax.axis_index("core")
    columns = [(xi + k) % x_size for k in range(x_size)]
    return jnp.stack([x * CORES + ci for x in columns] + [x * CORES + 1 - ci for x in columns])


def halving_steps(z_size, y_size, order):
    y_steps = [("y", y_size, 1 << k) for k in range(y_size.bit_length() - 1)]
    z_steps = [("z", z_size, 1 << k) for k in range(z_size.bit_length() - 1)]
    return y_steps + z_steps if order == "y" else z_steps + y_steps


def add_low(a, b):
    return (a.astype(F32) + b.astype(F32)).astype(BF)


def halve_kernel(info, keep, got, stays, goes):
    half = stays.shape[0]
    for b in range(keep.shape[0]):
        total = keep[b].astype(F32) + got[b].astype(F32)
        if b < half:
            stays[b] = total.astype(BF)
        else:
            goes[b - half] = total.astype(BF)


def halve(info, keep, got, after):
    shape = ((keep.shape[0] // 2,) + keep.shape[1:], BF)
    return call(halve_kernel, [info, keep, got], [shape, shape], name="halve", after=after)


def add_kernel(info, a, b, out):
    for k in range(out.shape[0]):
        out[k] = (a[k].astype(F32) + b[k].astype(F32)).astype(BF)


def add(info, a, b, after):
    return call(add_kernel, [info, a, b], [(a.shape, BF)], name="add", after=after)[0]


def reduce_scatter(info, keep, give, z_size, y_size, order, gates=None, steps=None):
    steps = steps or halving_steps(z_size, y_size, order)
    later = []
    for k, step in enumerate(steps):
        got = exchange(give, *step)
        if k < len(steps) - 1:
            keep, give = halve(info, keep, got, gates[k] if gates else ())
            later.append(give)
    return add_low(keep, got)[0], later


def gather_blocks(block, z_size, y_size, order):
    pieces = [block[None]]
    for step in halving_steps(z_size, y_size, order)[::-1]:
        whole_piece = pieces[0] if len(pieces) == 1 else jnp.concatenate(pieces, axis=0)
        pieces = [whole_piece, exchange(whole_piece, *step)]
    return pieces


def all_reduce(values, z_size, y_size):
    for step in halving_steps(z_size, y_size, "y"):
        values = add_low(values, exchange(values, *step))
    return values


def shards(
    z_size, y_size, x_size,
    token_ids, token_used, paired_ids, features, incoming, query_tokens, table, positions,
    emb_gain, emb_bias, qkv, out_weight, self_gain, self_bias, cross_query, key_shard,
    value_shard, cross_out, cross_gain, cross_bias, query_up, query_down, query_gain, query_bias,
    text_up, text_down, text_gain, text_bias, image_proj, text_proj, sharpness,
):
    group, slots = token_ids.shape
    queries, width = query_tokens.shape
    emb = image_proj.shape[1]
    items = group // CORES
    patch_size = x_size * CORES
    table_rows = table.shape[0]
    feat_rows = features.shape[1]
    kv_rows = key_shard.shape[0]
    dp_size = z_size * y_size
    xi, ci = lax.axis_index("x"), lax.axis_index("core")
    di = lax.axis_index("z") * y_size + lax.axis_index("y")
    member = xi * CORES + ci
    other = xi * CORES + 1 - ci
    block_rows = width // dp_size
    shared = block_rows % (8 * patch_size) == 0
    share_rows = block_rows // patch_size if shared else block_rows
    share, partner = (member, other) if shared else (jnp.int32(0), jnp.int32(0))
    info = jnp.stack([di, share, partner, ci, member, other]).astype(jnp.int32)
    places = patch_places(x_size).astype(jnp.int32)
    orders = {k: order_weights(z_size, y_size, k) for k in ("y", "z")}

    p = dict(
        emb_gain=emb_gain, emb_bias=emb_bias, self_gain=self_gain, self_bias=self_bias,
        cross_gain=cross_gain, cross_bias=cross_bias, query_gain=query_gain,
        query_bias=query_bias, text_gain=text_gain, text_bias=text_bias, positions=positions, query_tokens=query_tokens, qkv=qkv, out=out_weight,
        cross_query=cross_query, cross_out=cross_out, query_up=query_up, query_down=query_down,
        text_up=text_up, text_down=text_down, image_proj=image_proj, text_proj=text_proj,
    )

    def own_first(values):
        return jnp.concatenate(
            [part(values, ci, items, 0), part(values, 1 - ci, items, 0)], axis=0
        )

    local_ids = (own_first(token_ids) - member * table_rows).reshape(-1, 1)
    words_mine, words_give = look_up(info, local_ids, table)
    word_sum = words_mine + swap_core(words_give)
    words = [word_sum] + [from_x(word_sum, x_size, k) for k in range(1, x_size)]

    feat_mine = part(features, ci, items, 0)
    feat_got = swap_core(part(features, 1 - ci, items, 0))
    feats_x = [from_x(feat_mine, x_size, k) for k in range(1, x_size)]
    feat_late, key_late, value_late = stage(
        info, [feat_got, key_shard, value_shard], [word_sum]
    )
    feats = [feat_mine, feat_got]
    for k in range(1, x_size):
        feats += [feats_x[k - 1], from_x(feat_late, x_size, k)]
    key_x = [from_x(key_late, x_size, k) for k in range(1, x_size)]
    value_x = [from_x(value_late, x_size, k) for k in range(1, x_size)]

    used = jnp.concatenate(
        [jnp.ones((items, queries), jnp.int32), part(token_used, ci, items, 0)], axis=1
    ).reshape(items // 2, 2 * (queries + slots))
    (packed, probs, normal_q, normal_t, scale_q, scale_t, cross_q, lhs_mine, lhs_give, chosen_q) = (
        self_forward(info, words, used, p, orders, share_rows)
    )
    lhs_got = swap_core(lhs_give)
    held = list(stage(info, key_x + value_x, [packed]))
    own_keys, own_values = [key_shard] + held[: x_size - 1], [value_shard] + held[x_size - 1 :]
    kv_shards = own_keys + [swap_core(v) for v in own_keys]
    kv_shards += own_values + [swap_core(v) for v in own_values]
    text_names = ("text_up", "text_down", "text_gain", "text_bias", "text_proj")
    query_names = ("query_up", "query_down", "query_gain", "query_bias", "image_proj")
    (t_slope, t_keep, t_give, t_normal, t_scale, text_final, text_raw) = ff_forward(
        info, normal_t, p["self_gain"], p["self_bias"], text_names, p, orders["y"], share_rows,
        items, False,
    )
    t_got = swap_core(t_give)
    keys, values = key_value(info, places, feats, kv_shards, [t_normal])
    cross_probs, normal_c, scale_c, mixed_mine, mixed_give = cross_forward(
        info, cross_q, keys, values, normal_q, p, orders, share_rows
    )
    mixed_got = swap_core(mixed_give)
    (q_slope, q_keep, q_give, q_normal, q_scale, query_final, image_raw) = ff_forward(
        info, normal_c, p["cross_gain"], p["cross_bias"], query_names, p, orders["z"], share_rows,
        items, True,
    )
    q_got = swap_core(q_give)

    query_other, text_other = swap_core(query_final), swap_core(text_final)
    hidden_out = hidden_assemble(
        info, query_final, text_final, query_other, text_other, items
    )

    own_ids = jnp.concatenate(
        [part(token_ids, ci, items, 0), part(paired_ids, ci, items, 0)[:, None]], axis=1
    ).astype(F32)
    own_ids = jnp.pad(own_ids, ((0, 0), (0, 128 - own_ids.shape[1])))
    gathered = gather_doubling(
        jnp.concatenate([image_raw, text_raw, own_ids], axis=1), "core", CORES
    )
    gathered = gather_doubling(gather_doubling(gathered, "y", y_size), "z", z_size)
    loss, grad_image, grad_text, grad_sharp = contrast(
        info, gathered, sharpness.reshape(1, 1), queries, slots, group, emb, [hidden_out]
    )
    ids = gathered[:, 2 * emb : 2 * emb + slots].astype(jnp.int32)
    all_tokens = ids.reshape(dp_size, group * slots)

    q_rhs, grad_second, q_vectors = ff_backward(
        info, incoming, 0, grad_image, (q_slope, q_normal, q_scale),
        ("query_up", "query_down", "query_gain", "image_proj"), p, True,
    )
    t_rhs, grad_text_rows, t_vectors = ff_backward(
        info, incoming, 1, grad_text, (t_slope, t_normal, t_scale),
        ("text_up", "text_down", "text_gain", "text_proj"), p, False,
        [q_vectors, q_got, t_got, lhs_got, mixed_got],
    )
    q_weights = ff_weights(
        info, q_keep, q_got, q_rhs, swap_core(q_rhs), share_rows, dp_size, width, [t_vectors]
    )
    t_weights = ff_weights(
        info, t_keep, t_got, t_rhs, swap_core(t_rhs), share_rows, dp_size, width, [q_weights[0]]
    )

    y_first, z_first = (halving_steps(z_size, y_size, k) for k in ("y", "z"))

    m_rhs, grad_keys, grad_values, grad_query_rows, c_vectors = cross_backward(
        info, grad_second, normal_c, scale_c, keys, values, cross_probs, cross_q, p,
        [t_weights[0]],
    )
    m_got = swap_core(m_rhs)

    more = jnp.concatenate([c_vectors, q_vectors, t_vectors], axis=0)
    l_rhs, words_low = self_backward(
        info, grad_query_rows, grad_text_rows, (normal_q, normal_t, scale_q, scale_t), packed,
        probs, words, more, p, [],
    )
    t_more = halve(info, t_weights[0], exchange(t_weights[1], *y_first[0]), [words_low])
    q_more = halve(info, q_weights[0], exchange(q_weights[1], *z_first[0]), [t_more[1]])
    (words_low,) = stage(info, [words_low], [q_more[1]])
    words_other = swap_core(words_low)
    slot_of, rows_of, most = slots_of(info, all_tokens, table_rows, patch_size, [words_low])

    own = collect(info, slot_of, words_low, words_other, [q_more[1]])
    table_start = [own]
    own = gather_relative(own, "y", y_size)
    rising, falling = pass_on(own, "z", z_size)

    def few(words_low, words_other):
        return table_back(info, rows_of, own, rising, falling, z_size, y_size, table_rows)

    def many(words_low, words_other):
        low_core = ci == 0
        group_words = jnp.concatenate(
            [
                jnp.where(low_core, words_low, words_other),
                jnp.where(low_core, words_other, words_low),
            ],
            axis=0,
        )
        own = lax.dynamic_index_in_dim(all_tokens, di, axis=0, keepdims=False)
        rows = lax.broadcasted_iota(jnp.int32, (1, table_rows), 1) + member * table_rows
        hot = (own[:, None] == rows).astype(BF)
        return all_reduce(tn(hot, group_words).astype(BF), z_size, y_size).astype(F32)

    table_grad = lax.cond(most[0, 0] <= SLOTS, few, many, words_low, words_other)

    cuts = (2, dp_size // 2) if dp_size == 8 and kv_rows % 32 == 0 else (1, 1)
    kv_keep, kv_give = kv_weights(
        info, grad_keys, grad_values, feats, orders["y"], kv_rows, cuts,
        table_start,
    )

    mid = mid_weights(
        info, (lhs_mine, lhs_got), (mixed_mine, mixed_got), (m_rhs, m_got),
        (query_final, query_other), (text_final, text_other), grad_image, grad_text, orders["y"],
        share_rows, [kv_keep],
    )
    last = last_weights(
        info, chosen_q, (lhs_mine, lhs_got), (l_rhs, swap_core(l_rhs)), mid, orders["y"],
        share_rows, [],
    )
    tail_sum, _ = reduce_scatter(
        info, *last, z_size, y_size, "y"
    )
    kv_part = add(info, kv_keep, swap_core(kv_give), [rising[0]])
    if cuts[0] > 1:
        half = dp_size // 2
        kv_block, _ = reduce_scatter(
            info, kv_part[:half], kv_part[half:], z_size, y_size, "y"
        )
        key_grad, value_grad = kv_assemble(
            info, gather_blocks(kv_block, z_size, y_size, "y"), orders["y"], cuts, width
        )
    else:
        kv_total = all_reduce(kv_part[0], z_size, y_size).astype(F32)
        key_grad, value_grad = kv_total[:, :width], kv_total[:, width:]
    feature_mine, feature_give = features_back(
        info, places, grad_keys, grad_values, kv_shards, feat_rows, [kv_keep]
    )
    features_grad = features_assemble(info, feature_mine, swap_core(feature_give))

    def spread(values):
        return gather_patch(values, x_size) if shared else [values]

    q_sum, _ = reduce_scatter(
        info, *q_more, z_size, y_size, "z", [[last[0]]] * len(z_first), z_first[1:]
    )
    t_sum, _ = reduce_scatter(
        info, *t_more, z_size, y_size, "y", [[last[0]]] * len(y_first), y_first[1:]
    )
    ff_parts = spread(jnp.concatenate([q_sum, t_sum], axis=0))
    spots = places if shared else jnp.zeros((1,), jnp.int32)
    query_up_grad, query_down_grad, text_up_grad, text_down_grad = ff_assemble(
        info, spots, ff_parts, share_rows
    )

    tail_parts = spread(tail_sum)
    (
        qkv_grad, out_grad, cross_query_grad, cross_out_grad, image_proj_grad, text_proj_grad,
        tokens_grad, position_grad, vectors,
    ) = tail_assemble(info, spots, tail_parts, share_rows, width, emb, queries)

    return (
        hidden_out, loss.reshape(-1), features_grad, tokens_grad, table_grad, position_grad,
        vectors[0], vectors[1], qkv_grad, out_grad, vectors[2], vectors[3], cross_query_grad,
        key_grad, value_grad, cross_out_grad, vectors[4], vectors[5], query_up_grad,
        query_down_grad, vectors[6], vectors[7], text_up_grad, text_down_grad, vectors[8],
        vectors[9], image_proj_grad, text_proj_grad, grad_sharp.reshape(()),
    )


def solution(mesh):
    dp_size = mesh.shape["dp"]
    y_size = 1 << ((dp_size.bit_length() - 2) // 2)
    z_size = dp_size // y_size
    x_size = mesh.shape["patch"] // CORES
    split = Mesh(
        mesh.devices.reshape(z_size, y_size, x_size, CORES), ("z", "y", "x", "core")
    )
    dp, patch = ("z", "y"), ("x", "core")
    placed = (
        [P(dp, None), P(dp, None), P(dp), P(dp, patch, None), P(dp, None, None), P()]
        + [P(patch, None)]
        + [P()] * 8
        + [P(patch, None)] * 2
        + [P()] * 14
    )
    out = (
        [P(dp, None, None), P(dp), P(dp, patch, None), P(None, dp), P(patch, None)]
        + [P(None, dp), P(dp), P(dp), P(dp, None), P(dp, None), P(dp), P(dp)]
        + [P(dp, None), P(patch, None), P(patch, None), P(dp, None), P(dp), P(dp)]
        + [P(dp, None), P(dp, None), P(dp), P(dp), P(dp, None), P(dp, None)]
        + [P(dp), P(dp), P(dp, None), P(dp, None), P()]
    )

    def body(*args):
        return shards(z_size, y_size, x_size, *args)

    return jax.shard_map(
        body, mesh=split, in_specs=tuple(placed), out_specs=tuple(out), check_vma=False
    )
```

profile of v0, /device:TPU:1, one launch (start us, length us, event | category | flops | bytes accessed | tf_op | source)
XLA Modules:
  0.0 392.1 jit_solution(10009594856648648200)
XLA Ops:
  0.7 2.5 constant_dynamic-slice_fusion.1
  6.1 8.4 %words.1 = (bf16[256,768]{1,0:T(8,128)(2,1)}, bf16[256,768]{1,0:T(8,128)(2,1)}) custom-call(s32[6]{0:T(128)S(1)} %stack.36.refs_0_, s32[512,1]{1,0:T(8,128)} %sub.36.refs_1_, bf16[3840,768]{1,0:T(8,128)(2,1)} %refs_2_.5), custom_call_target="tpu_custom_call" | custom-call | flops 1 | bytes 1 | tf_op jit(solution)/shard_map/words/pallas_call | solution.py:182
  15.0 1.6 collective-permute-done.3
  17.7 2.6 collective-permute-start.4
  20.3 2.7 stage.3
  26.2 3.5 collective-permute-done.4.refs_12_.refs_17_
  41.2 8.7 %self_forward.1 = (bf16[512,2304]{1,0:T(8,128)(2,1)S(1)}, bf16[12,512,128]{2,1,0:T(8,128)(2,1)S(1)}, f32[256,768]{1,0:T(8,128)S(1)}, f32[256,768]{1,0:T(8,128)S(...) custom-call(s32[6]{0:T(128)} %copy-done.107, ...), custom_call_target="tpu_custom_call" | custom-call | flops 1 | bytes 1 | tf_op jit(solution)/shard_map/self_forward/pallas_call | solution.py:182
  51.3 1.9 collective-permute-start.12
  53.1 2.2 stage.4
  58.9 11.4 %ff_forward.2 = (bf16[256,3072]{1,0:T(8,128)(2,1)}, bf16[960,256]{1,0:T(8,128)(2,1)}, bf16[960,256]{1,0:T(8,128)(2,1)}, f32[256,768]{1,0:T(8,128)}, f32[256,1]{1...) custom-call(s32[6]{0:T(128)S(1)} %copy-done.109, f32[256,768]{1,0:T(8,128)} %copy-done.33, f32[768]{0:T(1024)} %refs_7_.9, ...), custom_call_target="tpu_custom_call" | custom-call | flops 1 | bytes 1 | tf_op jit(solution)/shard_map/ff_forward/pallas_call | solution.py:182
  70.3 13.5 %collective-permute-done.7.refs_5_.refs_6_ = bf16[8,32,1408]{2,1,0:T(8,128)(2,1)} collective-permute-done((bf16[8,32,1408]{2,1,0:T(8,128)(2,1)}, bf16[8,32,1408]{2,1,0:T(8,128)(2,1)}, u32[]{:S(2)}, u32[]{:S(2)}) %collective-permute-start.7) | collective-permute-done | bytes 720928 | tf_op jit(solution)/shard_map/ppermute | solution.py:1420
  85.0 8.4 %key_value.1 = (bf16[8,128,768]{2,1,0:T(8,128)(2,1)S(1)}, bf16[8,128,768]{2,1,0:T(8,128)(2,1)S(1)}) custom-call(s32[6]{0:T(128)S(1)} %copy-done.109, s32[4]{0:T(128)S(1)} %pad_add_fusion.refs_1_, bf16[8,32,1408]{2,1,0:T(8,128)(2,1)} %get-tuple-element.278.refs_2_.refs_3_, bf16[8,32,1408]{2,1,0:T(8,128)(2,1)} %collective-permute-done.5.refs_1_.refs_3_.refs_4_, ...), custom_call_target="tpu_custom_call" | custom-call | flops 1 | bytes 1 | tf_op jit(solution)/shard_map/key_value/pallas_call | solution.py:182
  93.6 3.4 cross_forward.1
  100.7 11.2 %ff_forward.3 = (bf16[256,3072]{1,0:T(8,128)(2,1)}, bf16[960,256]{1,0:T(8,128)(2,1)}, bf16[960,256]{1,0:T(8,128)(2,1)}, f32[256,768]{1,0:T(8,128)}, f32[256,1]{1...) custom-call(s32[6]{0:T(128)S(1)} %copy-done.109, f32[256,768]{1,0:T(8,128)} %copy-done.35, f32[768]{0:T(1024)} %refs_4_.8, ...), custom_call_target="tpu_custom_call" | custom-call | flops 1 | bytes 1 | tf_op jit(solution)/shard_map/ff_forward/pallas_call | solution.py:182
  117.1 1.5 collective-permute-start.17
  118.6 1.7 collective-permute-done.17
  122.4 1.5 collective-permute-start.18
  123.9 2.1 collective-permute-done.18
  127.6 2.5 collective-permute-start.19
  130.1 2.9 collective-permute-start.15
  133.6 1.8 collective-permute-done.19
  136.1 3.4 collective-permute-start.22
  141.9 2.6 hidden_assemble.1.refs_3_
  145.9 1.9 contrast.1
  148.3 9.9 %ff_backward.2 = (bf16[256,3840]{1,0:T(8,128)(2,1)}, f32[256,768]{1,0:T(8,128)}, f32[2,768]{1,0:T(2,128)}) custom-call(s32[6]{0:T(128)S(1)} %copy-done.109, bf16[16,64,768]{2,1,0:T(8,128)(2,1)} %refs_1_.5, bf16[16,256]{1,0:T(8,128)(2,1)} %copy-done.84, bf16[768,256]{1,0:T(8,128)(2,1)} %refs_3_.10, f32[256,768]{1,0:T(8,128)} %get-tuple-element.197.refs_4_, ...), custom_call_target="tpu_custom_call" | custom-call | flops 1 | bytes 1 | tf_op jit(solution)/shard_map/ff_backward/pallas_call | solution.py:619
  158.4 18.4 %ff_backward.3 = (bf16[256,3840]{1,0:T(8,128)(2,1)}, f32[256,768]{1,0:T(8,128)}, f32[2,768]{1,0:T(2,128)}) custom-call(s32[6]{0:T(128)S(1)} %copy-done.109, bf16[16,64,768]{2,1,0:T(8,128)(2,1)} %refs_1_.5, bf16[16,256]{1,0:T(8,128)(2,1)} %copy-done.81, bf16[768,256]{1,0:T(8,128)(2,1)} %refs_3_.11, f32[256,768]{1,0:T(8,128)} %get-tuple-element.186.refs_14_.refs_4_, ...), custom_call_target="tpu_custom_call" | custom-call | flops 1 | bytes 1 | tf_op jit(solution)/shard_map/ff_backward/pallas_call | solution.py:619
  177.3 1.5 copy-done.38
  179.5 4.3 %ff_weights.2 = (bf16[4,192,768]{2,1,0:T(8,128)(2,1)S(1)}, bf16[4,192,768]{2,1,0:T(8,128)(2,1)}) custom-call(s32[6]{0:T(128)S(1)} %copy-done.109, bf16[960,256]{1,0:T(8,128)(2,1)S(1)} %copy-done.55, bf16[960,256]{1,0:T(8,128)(2,1)} %collective-permute-done.21.refs_11_.refs_2_, bf16[256,3840]{1,0:T(8,128)(2,1)S(1)} %copy-done.38, ...), custom_call_target="tpu_custom_call" | custom-call | flops 1 | bytes 1 | tf_op jit(solution)/shard_map/ff_weights/pallas_call | solution.py:182
  183.9 3.9 %ff_weights.3 = (bf16[4,192,768]{2,1,0:T(8,128)(2,1)S(1)}, bf16[4,192,768]{2,1,0:T(8,128)(2,1)}) custom-call(s32[6]{0:T(128)S(1)} %copy-done.109, bf16[960,256]{1,0:T(8,128)(2,1)S(1)} %copy-done.54, bf16[960,256]{1,0:T(8,128)(2,1)} %collective-permute-done.20.refs_12_.refs_2_, bf16[256,3840]{1,0:T(8,128)(2,1)S(1)} %copy-done.39, ...), custom_call_target="tpu_custom_call" | custom-call | flops 1 | bytes 1 | tf_op jit(solution)/shard_map/ff_weights/pallas_call | solution.py:182
  191.2 1.5 reshape.100.refs_1_
  204.7 9.1 %cross_backward.1 = (bf16[256,1536]{1,0:T(8,128)(2,1)S(1)}, bf16[8,128,768]{2,1,0:T(8,128)(2,1)S(1)}, bf16[8,128,768]{2,1,0:T(8,128)(2,1)S(1)}, f32[256,768]{1,0:T(8,128)S(1)}, f32[2,768]{1,0:T(2,128)S(1)}) custom-call(s32[6]{0:T(128)S(1)} %copy-done.109, f32[256,768]{1,0:T(8,128)S(1)} %copy-done.51, f32[256,768]{1,0:T(8,128)S(1)} %copy-done.36, ...), custom_call_target="tpu_custom_call" | custom-call | flops 1 | bytes 1 | tf_op jit(solution)/shard_map/cross_backward/pallas_call | solution.py:182
  214.0 10.9 %self_backward.1 = (bf16[304,3840]{1,0:T(8,128)(2,1)}, bf16[256,768]{1,0:T(8,128)(2,1)S(1)}) custom-call(s32[6]{0:T(128)S(1)} %copy-done.109, f32[256,768]{1,0:T(8,128)S(1)} %get-tuple-element.220.refs_1_, f32[256,768]{1,0:T(8,128)S(1)} %copy-done.52, f32[256,768]{1,0:T(8,128)S(1)} %copy-done.32, f32[256,768]{1,0:T(8,128)S(1)} %copy-done.34, ...), custom_call_target="tpu_custom_call" | custom-call | flops 1 | bytes 1 | tf_op jit(solution)/shard_map/self_backward/pallas_call | solution.py:182
  224.9 2.3 halve.8
  227.2 1.6 halve.9
  230.1 5.4 %slots.1 = (s32[8,512]{1,0:T(8,128)S(1)}, s32[1,1024]{1,0:T(1,128)}, s32[1,1]{1,0:T(1,128)}) custom-call(s32[6]{0:T(128)S(1)} %copy-done.109, s32[8,512]{1,0:T(8,128)S(1)} %copy-done.120, bf16[256,768]{1,0:T(8,128)(2,1)S(1)} %stage.5.refs_2_), custom_call_target="tpu_custom_call" | custom-call | flops 99999997952 | bytes 1 | tf_op jit(solution)/shard_map/slots/pallas_call | solution.py:182
  236.3 8.0 %kv_weights.1 = (bf16[8,176,384]{2,1,0:T(8,128)(2,1)S(1)}, bf16[8,176,384]{2,1,0:T(8,128)(2,1)S(1)}) custom-call(s32[6]{0:T(128)S(1)} %copy-done.109, bf16[8,128,768]{2,1,0:T(8,128)(2,1)S(1)} %get-tuple-element.218.refs_1_.refs_2_, bf16[8,128,768]{2,1,0:T(8,128)(2,1)S(1)} %get-tuple-element.219.refs_2_.refs_3_, ...), custom_call_target="tpu_custom_call" | custom-call | flops 1 | bytes 1 | tf_op jit(solution)/shard_map/kv_weights/pallas_call | solution.py:182
  245.5 5.1 %collective-permute-done.38 = bf16[128,768]{1,0:T(8,128)(2,1)S(1)} collective-permute-done((bf16[128,768]{1,0:T(8,128)(2,1)S(1)}, bf16[128,768]{1,0:T(8,128)(2,1)S(1)}, u32[]{:S(2)}, u32[]{:S(2)}) %collective-permute-start.38) | collective-permute-done | bytes 196640 | tf_op jit(solution)/shard_map/ppermute | solution.py:1428
  250.6 3.0 collective-permute-start.39
  253.6 1.6 collective-permute-start.30
  255.2 2.3 collective-permute-start.54
  257.6 3.2 collective-permute-done.39.refs_3_
  260.7 4.3 %collective-permute-start.52 = (bf16[2,192,768]{2,1,0:T(8,128)(2,1)S(1)}, bf16[2,192,768]{2,1,0:T(8,128)(2,1)}, u32[]{:S(2)}, u32[]{:S(2)}) collective-permute-start(bf16[2,192,768]{2,1,0:T(8,128)(2,1)S(1)} %get-tuple-element.230.refs_2_.refs_4_), channel_id=1, source_target_pairs={{0,16},{8,24},{16,0},{24,8},{1,17},{9,25},{17,1},{25,9},{2,18},{10... | collective-permute-start | bytes 1769480 | tf_op jit(solution)/shard_map/ppermute | solution.py:1428
  268.1 4.3 %mid_weights.1.refs_6_ = bf16[8,48,1024]{2,1,0:T(8,128)(2,1)} custom-call(s32[6]{0:T(128)S(1)} %copy-done.109, bf16[192,1024]{1,0:T(8,128)(2,1)} %copy-done.56, bf16[192,1024]{1,0:T(8,128)(2,1)} %collective-permute-done.22.refs_13_.refs_2_.refs_3_, bf16[192,256]{1,0:T(8,128)(2,1)} %copy-done.88, bf16[192,256]{1,0:T(8,128)(2,1)} %collective-permute-done.23.refs_14_.refs_4_, ...), custom_call_target="tpu_custom_call" | custom-call | flops 99999997952 | bytes 1 | tf_op jit(solution)/shard_map/mid_weights/pallas_call | solution.py:182
  275.3 3.2 last_weights.1
  282.5 5.4 %collective-permute-start.55 = (bf16[1,192,768]{2,1,0:T(8,128)(2,1)S(1)}, bf16[1,192,768]{2,1,0:T(8,128)(2,1)S(1)}, u32[]{:S(2)}, u32[]{:S(2)}) collective-permute-start(bf16[1,192,768]{2,1,0:T(8,128)(2,1)S(1)} %get-tuple-element.267), channel_id=1, source_target_pairs={{0,16},{8,24},{16,0},{24,8},{1,17},{9,25},{17,1},{25,9},{2,18},{10... | collective-permute-start | bytes 884744 | tf_op jit(solution)/shard_map/ppermute | solution.py:1428
  292.8 5.7 %collective-permute-done.42 = bf16[256,768]{1,0:T(8,128)(2,1)S(1)} collective-permute-done((bf16[256,768]{1,0:T(8,128)(2,1)S(1)}, bf16[256,768]{1,0:T(8,128)(2,1)S(1)}, u32[]{:S(2)}, u32[]{:S(2)}) %collective-permute-start.42) | collective-permute-done | bytes 393248 | tf_op jit(solution)/shard_map/ppermute | solution.py:1458
  298.5 8.4 %collective-permute-start.40 = (bf16[256,768]{1,0:T(8,128)(2,1)S(1)}, bf16[256,768]{1,0:T(8,128)(2,1)}, u32[]{:S(2)}, u32[]{:S(2)}) collective-permute-start(bf16[256,768]{1,0:T(8,128)(2,1)S(1)} %copy-done.99), channel_id=1, source_target_pairs={{0,8},{8,16},{16,24},{1,9},{9,17},{17,25},{2,10},{10,18},{18,26},{... | collective-permute-start | bytes 1179656 | tf_op jit(solution)/shard_map/ppermute | solution.py:1457
  306.9 3.4 collective-permute-done.55
  314.6 2.2 collective-permute-start.33
  316.8 4.9 %collective-permute-done.48 = bf16[1,176,384]{2,1,0:T(8,128)(2,1)S(1)} collective-permute-done((bf16[1,176,384]{2,1,0:T(8,128)(2,1)S(1)}, bf16[1,176,384]{2,1,0:T(8,128)(2,1)S(1)}, u32[]{:S(2)}, u32[]{:S(2)}) %collective-permute-start.48) | collective-permute-done | bytes 135200 | tf_op jit(solution)/shard_map/ppermute | solution.py:1428
  321.8 2.8 collective-permute-start.41
  325.9 5.4 %collective-permute-done.49 = bf16[1,176,384]{2,1,0:T(8,128)(2,1)S(1)} collective-permute-done((bf16[1,176,384]{2,1,0:T(8,128)(2,1)S(1)}, bf16[1,176,384]{2,1,0:T(8,128)(2,1)S(1)}, u32[]{:S(2)}, u32[]{:S(2)}) %collective-permute-start.49) | collective-permute-done | bytes 135200 | tf_op jit(solution)/shard_map/ppermute | solution.py:1428
  332.1 4.4 %collective-permute-start.50 = (bf16[2,176,384]{2,1,0:T(8,128)(2,1)}, bf16[2,176,384]{2,1,0:T(8,128)(2,1)}, u32[]{:S(2)}, u32[]{:S(2)}) collective-permute-start(bf16[2,176,384]{2,1,0:T(8,128)(2,1)} %pad_maximum_fusion.4), channel_id=1, source_target_pairs={{0,8},{8,0},{16,24},{24,16},{1,9},{9,1},{17,25},{25,17},{2,10},{10... | collective-permute-start | bytes 811016 | tf_op jit(solution)/shard_map/ppermute | solution.py:1428
  338.5 6.1 %features_back.1 = (f32[8,32,1408]{2,1,0:T(8,128)S(1)}, bf16[8,32,1408]{2,1,0:T(8,128)(2,1)}) custom-call(s32[6]{0:T(128)S(1)} %copy-done.109, s32[4]{0:T(128)S(1)} %copy-done.79, bf16[8,128,768]{2,1,0:T(8,128)(2,1)S(1)} %copy-done.9, bf16[8,128,768]{2,1,0:T(8,128)(2,1)S(1)} %copy-done.11, bf16[352,768]{1,0:T(8,128)(2,1)} %refs_4_.9, ...), custom_call_target="tpu_custom_call" | custom-call | flops 1 | bytes 1 | tf_op jit(solution)/shard_map/features_back/pallas_call | solution.py:182
  345.7 7.9 %collective-permute-start.29 = (bf16[8,32,1408]{2,1,0:T(8,128)(2,1)}, bf16[8,32,1408]{2,1,0:T(8,128)(2,1)}, u32[]{:S(2)}, u32[]{:S(2)}) collective-permute-start(bf16[8,32,1408]{2,1,0:T(8,128)(2,1)} %get-tuple-element.234), channel_id=1, source_target_pairs={{0,1},{1,0},{2,3},{3,2},{4,5},{5,4},{6,7},{7,6},{8,9},{9,8},{10,11... | collective-permute-start | bytes 2162696 | tf_op jit(solution)/shard_map/ppermute | solution.py:1416
  353.7 10.5 %conditional.1 = (f32[3840,768]{1,0:T(8,128)}) conditional(s32[]{:T(128)} %bitcast.12, (s32[]{:T(128)}, s32[8,512]{1,0:T(8,128)S(1)}, s32[]{:T(128)}, s32[]{:T(128)}, bf16[256,768]{1,0:T(8,128)(2,1)S(1)}, /*index=5*/bf16[256,768]{1,0:T(8,128)(2,1)S(1)}) %tuple.43, (s32[6]{0:T(128)S(1)}, s32[1,1024]{1,0:T(1,128)S(1)}, bf16[256,768]{1,0:T(8,128)(2,1)S(1)}, ...), branch_computations={%region_0.1_spmd, %region_1.2_spmd} | conditional | flops 3065122560 | bytes 161648864 | solution.py:1695
  353.9 10.3 %table.1 = f32[3840,768]{1,0:T(8,128)} custom-call(s32[6]{0:T(128)S(1)} %get-tuple-element.39.refs_0_, s32[1,1024]{1,0:T(1,128)S(1)} %get-tuple-element.40.refs_1_, bf16[256,768]{1,0:T(8,128)(2,1)S(1)} %get-tuple-element.41.refs_2_, bf16[256,768]{1,0:T(8,128)(2,1)S(1)} %get-tuple-element.42.refs_3_, bf16[256,768]{1,0:T(8,128)(2,1)} %get-tuple-element.43.refs_4_, ...), custom_call_target="tpu_custom_call" | custom-call | flops 1 | bytes 1 | tf_op jit(solution)/shard_map/cond/branch_1_fun/table/pallas_call | solution.py:182
  364.2 3.9 collective-permute-start.57
  372.9 5.0 %collective-permute-done.35.refs_3_ = bf16[48,2688]{1,0:T(8,128)(2,1)S(1)} collective-permute-done((bf16[48,2688]{1,0:T(8,128)(2,1)S(1)}, bf16[48,2688]{1,0:T(8,128)(2,1)S(1)}, u32[]{:S(2)}, u32[]{:S(2)}) %collective-permute-start.35) | collective-permute-done | bytes 258080 | tf_op jit(solution)/shard_map/ppermute | solution.py:1420
  377.9 1.5 collective-permute-start.37
  380.0 3.2 features_assemble.1
  383.2 3.0 ff_assemble.1
  386.2 2.6 kv_assemble.1
  388.9 2.4 tail_assemble.1
  (371 shorter events, 91.9 us)
Async XLA Ops:
  0.7 57.2 %copy-start = (s32[16]{0:T(128)S(1)}, s32[16]{0:T(128)}, u32[]{:S(2)}) copy-start(s32[16]{0:T(128)} %param.35) | copy-start | bytes 196
  3.3 17.1 %collective-permute-start.5 = (bf16[8,32,1408]{2,1,0:T(8,128)(2,1)}, bf16[8,32,1408]{2,1,0:T(8,128)(2,1)}, u32[]{:S(2)}, u32[]{:S(2)}) collective-permute-start(bf16[8,32,1408]{2,1,0:T(8,128)(2,1)} %get-tuple-element.277), channel_id=1, source_target_pairs={{0,1},{1,0},{2,3},{3,2},{4,5},{5,4},{6,7},{7,6},{8,9},{9,8},{10,11... | collective-permute-start | bytes 2162696 | tf_op jit(solution)/shard_map/ppermute | solution.py:1416
  6.1 27.6 %copy-start.2 = (bf16[768,2304]{1,0:T(8,128)(2,1)S(1)}, bf16[768,2304]{1,0:T(8,128)(2,1)}, u32[]{:S(2)}) copy-start(bf16[768,2304]{1,0:T(8,128)(2,1)} %refs_14_.1) | copy-start | bytes 10616836
  14.5 2.1 collective-permute-start.3
  17.7 12.0 %collective-permute-start.4 = (bf16[256,768]{1,0:T(8,128)(2,1)S(1)}, bf16[256,768]{1,0:T(8,128)(2,1)S(1)}, u32[]{:S(2)}, u32[]{:S(2)}) collective-permute-start(bf16[256,768]{1,0:T(8,128)(2,1)S(1)} %add.91.refs_11_.refs_4_.refs_16_), channel_id=1, source_target_pairs={{0,2},{2,0},{1,3},{3,1},{4,6},{6,4},{5,7},{7,5},{8,10},{10,8},{9,1... | collective-permute-start | bytes 1179656 | tf_op jit(solution)/shard_map/ppermute | solution.py:1420
  23.8 27.5 %collective-permute-start.8 = (bf16[352,768]{1,0:T(8,128)(2,1)}, bf16[352,768]{1,0:T(8,128)(2,1)}, u32[]{:S(2)}, u32[]{:S(2)}) collective-permute-start(bf16[352,768]{1,0:T(8,128)(2,1)} %get-tuple-element.180), channel_id=1, source_target_pairs={{0,2},{2,0},{1,3},{3,1},{4,6},{6,4},{5,7},{7,5},{8,10},{10,8},{9,1... | collective-permute-start | bytes 1622024 | tf_op jit(solution)/shard_map/ppermute | solution.py:1420
  23.8 29.3 %collective-permute-start.9 = (bf16[352,768]{1,0:T(8,128)(2,1)}, bf16[352,768]{1,0:T(8,128)(2,1)}, u32[]{:S(2)}, u32[]{:S(2)}) collective-permute-start(bf16[352,768]{1,0:T(8,128)(2,1)} %get-tuple-element.181), channel_id=1, source_target_pairs={{0,2},{2,0},{1,3},{3,1},{4,6},{6,4},{5,7},{7,5},{8,10},{10,8},{9,1... | collective-permute-start | bytes 1622024 | tf_op jit(solution)/shard_map/ppermute | solution.py:1420
  25.2 32.5 %collective-permute-start.10 = (bf16[352,768]{1,0:T(8,128)(2,1)}, bf16[352,768]{1,0:T(8,128)(2,1)}, u32[]{:S(2)}, u32[]{:S(2)}) collective-permute-start(bf16[352,768]{1,0:T(8,128)(2,1)} %refs_4_.9), channel_id=1, source_target_pairs={{0,1},{1,0},{2,3},{3,2},{4,5},{5,4},{6,7},{7,6},{8,9},{9,8},{10,11... | collective-permute-start | bytes 1622024 | tf_op jit(solution)/shard_map/ppermute | solution.py:1416
  26.2 44.1 %collective-permute-start.6 = (bf16[8,32,1408]{2,1,0:T(8,128)(2,1)}, bf16[8,32,1408]{2,1,0:T(8,128)(2,1)}, u32[]{:S(2)}, u32[]{:S(2)}) collective-permute-start(bf16[8,32,1408]{2,1,0:T(8,128)(2,1)} %get-tuple-element.278.refs_2_.refs_3_), channel_id=1, source_target_pairs={{0,2},{2,0},{1,3},{3,1},{4,6},{6,4},{5,7},{7,5},{8,10},{10,8},{9,1... | collective-permute-start | bytes 2162696 | tf_op jit(solution)/shard_map/ppermute | solution.py:1420
  30.5 53.4 %collective-permute-start.7 = (bf16[8,32,1408]{2,1,0:T(8,128)(2,1)}, bf16[8,32,1408]{2,1,0:T(8,128)(2,1)}, u32[]{:S(2)}, u32[]{:S(2)}) collective-permute-start(bf16[8,32,1408]{2,1,0:T(8,128)(2,1)} %get-tuple-element.179), channel_id=1, source_target_pairs={{0,2},{2,0},{1,3},{3,1},{4,6},{6,4},{5,7},{7,5},{8,10},{10,8},{9,1... | collective-permute-start | bytes 2162696 | tf_op jit(solution)/shard_map/ppermute | solution.py:1420
  51.3 19.1 %collective-permute-start.12 = (bf16[352,768]{1,0:T(8,128)(2,1)}, bf16[352,768]{1,0:T(8,128)(2,1)}, u32[]{:S(2)}, u32[]{:S(2)}) collective-permute-start(bf16[352,768]{1,0:T(8,128)(2,1)} %refs_8_.13), channel_id=1, source_target_pairs={{0,1},{1,0},{2,3},{3,2},{4,5},{5,4},{6,7},{7,6},{8,9},{9,8},{10,11... | collective-permute-start | bytes 1622024 | tf_op jit(solution)/shard_map/ppermute | solution.py:1416
  56.8 27.1 %collective-permute-start.11 = (bf16[352,768]{1,0:T(8,128)(2,1)}, bf16[352,768]{1,0:T(8,128)(2,1)}, u32[]{:S(2)}, u32[]{:S(2)}) collective-permute-start(bf16[352,768]{1,0:T(8,128)(2,1)} %get-tuple-element.183.refs_7_.refs_5_), channel_id=1, source_target_pairs={{0,1},{1,0},{2,3},{3,2},{4,5},{5,4},{6,7},{7,6},{8,9},{9,8},{10,11... | collective-permute-start | bytes 1622024 | tf_op jit(solution)/shard_map/ppermute | solution.py:1416
  57.7 26.1 %collective-permute-start.13 = (bf16[352,768]{1,0:T(8,128)(2,1)}, bf16[352,768]{1,0:T(8,128)(2,1)}, u32[]{:S(2)}, u32[]{:S(2)}) collective-permute-start(bf16[352,768]{1,0:T(8,128)(2,1)} %get-tuple-element.184.refs_11_.refs_9_), channel_id=1, source_target_pairs={{0,1},{1,0},{2,3},{3,2},{4,5},{5,4},{6,7},{7,6},{8,9},{9,8},{10,11... | collective-permute-start | bytes 1622024 | tf_op jit(solution)/shard_map/ppermute | solution.py:1416
  58.1 25.8 %copy-start.78 = (s32[4]{0:T(128)}, s32[4]{0:T(128)S(1)}, u32[]{:S(2)}) copy-start(s32[4]{0:T(128)S(1)} %pad_add_fusion.refs_1_) | copy-start | bytes 52
  113.2 1.9 collective-permute-start.16
  117.1 3.2 collective-permute-start.17
  122.4 3.7 collective-permute-start.18
  127.6 7.8 %collective-permute-start.19 = (f32[64,640]{1,0:T(8,128)S(1)}, f32[64,640]{1,0:T(8,128)S(1)}, u32[]{:S(2)}, u32[]{:S(2)}) collective-permute-start(f32[64,640]{1,0:T(8,128)S(1)} %pad_maximum_fusion.5), channel_id=1, source_target_pairs={{0,16},{8,24},{16,0},{24,8},{1,17},{9,25},{17,1},{25,9},{2,18},{10... | collective-permute-start | bytes 491528 | tf_op jit(solution)/shard_map/ppermute | solution.py:1428
  130.1 11.0 %collective-permute-start.15 = (bf16[256,768]{1,0:T(8,128)(2,1)}, bf16[256,768]{1,0:T(8,128)(2,1)}, u32[]{:S(2)}, u32[]{:S(2)}) collective-permute-start(bf16[256,768]{1,0:T(8,128)(2,1)} %get-tuple-element.192.refs_2_.refs_9_), channel_id=1, source_target_pairs={{0,1},{1,0},{2,3},{3,2},{4,5},{5,4},{6,7},{7,6},{8,9},{9,8},{10,11... | collective-permute-start | bytes 1179656 | tf_op jit(solution)/shard_map/ppermute | solution.py:1416
  133.0 25.3 %collective-permute-start.20 = (bf16[960,256]{1,0:T(8,128)(2,1)}, bf16[960,256]{1,0:T(8,128)(2,1)}, u32[]{:S(2)}, u32[]{:S(2)}) collective-permute-start(bf16[960,256]{1,0:T(8,128)(2,1)} %get-tuple-element.204), channel_id=1, source_target_pairs={{0,1},{1,0},{2,3},{3,2},{4,5},{5,4},{6,7},{7,6},{8,9},{9,8},{10,11... | collective-permute-start | bytes 1474568 | tf_op jit(solution)/shard_map/ppermute | solution.py:1416
  133.1 25.3 %collective-permute-start.21 = (bf16[960,256]{1,0:T(8,128)(2,1)}, bf16[960,256]{1,0:T(8,128)(2,1)}, u32[]{:S(2)}, u32[]{:S(2)}) collective-permute-start(bf16[960,256]{1,0:T(8,128)(2,1)} %get-tuple-element.209), channel_id=1, source_target_pairs={{0,1},{1,0},{2,3},{3,2},{4,5},{5,4},{6,7},{7,6},{8,9},{9,8},{10,11... | collective-permute-start | bytes 1474568 | tf_op jit(solution)/shard_map/ppermute | solution.py:1416
  133.6 8.3 %collective-permute-start.14 = (bf16[256,768]{1,0:T(8,128)(2,1)}, bf16[256,768]{1,0:T(8,128)(2,1)}, u32[]{:S(2)}, u32[]{:S(2)}) collective-permute-start(bf16[256,768]{1,0:T(8,128)(2,1)} %get-tuple-element.191.refs_1_.refs_7_), channel_id=1, source_target_pairs={{0,1},{1,0},{2,3},{3,2},{4,5},{5,4},{6,7},{7,6},{8,9},{9,8},{10,11... | collective-permute-start | bytes 1179656 | tf_op jit(solution)/shard_map/ppermute | solution.py:1416
  136.1 22.3 %collective-permute-start.22 = (bf16[192,1024]{1,0:T(8,128)(2,1)}, bf16[192,1024]{1,0:T(8,128)(2,1)}, u32[]{:S(2)}, u32[]{:S(2)}) collective-permute-start(bf16[192,1024]{1,0:T(8,128)(2,1)} %copy-done.87), channel_id=1, source_target_pairs={{0,1},{1,0},{2,3},{3,2},{4,5},{5,4},{6,7},{7,6},{8,9},{9,8},{10,11... | collective-permute-start | bytes 1179656 | tf_op jit(solution)/shard_map/ppermute | solution.py:1416
  141.2 17.2 %collective-permute-start.23 = (bf16[192,256]{1,0:T(8,128)(2,1)}, bf16[192,256]{1,0:T(8,128)(2,1)}, u32[]{:S(2)}, u32[]{:S(2)}) collective-permute-start(bf16[192,256]{1,0:T(8,128)(2,1)} %copy-done.89), channel_id=1, source_target_pairs={{0,1},{1,0},{2,3},{3,2},{4,5},{5,4},{6,7},{7,6},{8,9},{9,8},{10,11... | collective-permute-start | bytes 294920 | tf_op jit(solution)/shard_map/ppermute | solution.py:1416
  158.2 19.0 %collective-permute-start.25 = (bf16[256,3840]{1,0:T(8,128)(2,1)}, bf16[256,3840]{1,0:T(8,128)(2,1)}, u32[]{:S(2)}, u32[]{:S(2)}) collective-permute-start(bf16[256,3840]{1,0:T(8,128)(2,1)} %get-tuple-element.214.refs_3_), channel_id=1, source_target_pairs={{0,1},{1,0},{2,3},{3,2},{4,5},{5,4},{6,7},{7,6},{8,9},{9,8},{10,11... | collective-permute-start | bytes 5898248 | tf_op jit(solution)/shard_map/ppermute | solution.py:1416
  176.7 7.1 %collective-permute-start.24 = (bf16[256,3840]{1,0:T(8,128)(2,1)}, bf16[256,3840]{1,0:T(8,128)(2,1)S(1)}, u32[]{:S(2)}, u32[]{:S(2)}) collective-permute-start(bf16[256,3840]{1,0:T(8,128)(2,1)} %get-tuple-element.212.refs_3_), channel_id=1, source_target_pairs={{0,1},{1,0},{2,3},{3,2},{4,5},{5,4},{6,7},{7,6},{8,9},{9,8},{10,11... | collective-permute-start | bytes 5898248 | tf_op jit(solution)/shard_map/ppermute | solution.py:1416
  188.8 36.1 %collective-permute-start.27 = (bf16[4,192,768]{2,1,0:T(8,128)(2,1)}, bf16[4,192,768]{2,1,0:T(8,128)(2,1)}, u32[]{:S(2)}, u32[]{:S(2)}) collective-permute-start(bf16[4,192,768]{2,1,0:T(8,128)(2,1)} %get-tuple-element.228), channel_id=1, source_target_pairs={{0,4},{4,0},{1,5},{5,1},{2,6},{6,2},{3,7},{7,3},{8,12},{12,8},{9,1... | collective-permute-start | bytes 3538952 | tf_op jit(solution)/shard_map/ppermute | solution.py:1428
  190.1 37.1 %collective-permute-start.26 = (bf16[4,192,768]{2,1,0:T(8,128)(2,1)}, bf16[4,192,768]{2,1,0:T(8,128)(2,1)}, u32[]{:S(2)}, u32[]{:S(2)}) collective-permute-start(bf16[4,192,768]{2,1,0:T(8,128)(2,1)} %get-tuple-element.227), channel_id=1, source_target_pairs={{0,8},{8,0},{16,24},{24,16},{1,9},{9,1},{17,25},{25,17},{2,10},{10... | collective-permute-start | bytes 3538952 | tf_op jit(solution)/shard_map/ppermute | solution.py:1428
  213.8 30.9 %copy-start.86 = (bf16[256,1536]{1,0:T(8,128)(2,1)}, bf16[256,1536]{1,0:T(8,128)(2,1)S(1)}, u32[]{:S(2)}) copy-start(bf16[256,1536]{1,0:T(8,128)(2,1)S(1)} %get-tuple-element.239.refs_5_) | copy-start | bytes 2359300
  229.4 6.1 %collective-permute-start.28 = (bf16[256,768]{1,0:T(8,128)(2,1)S(1)}, bf16[256,768]{1,0:T(8,128)(2,1)S(1)}, u32[]{:S(2)}, u32[]{:S(2)}) collective-permute-start(bf16[256,768]{1,0:T(8,128)(2,1)S(1)} %stage.5.refs_2_), channel_id=1, source_target_pairs={{0,1},{1,0},{2,3},{3,2},{4,5},{5,4},{6,7},{7,6},{8,9},{9,8},{10,11... | collective-permute-start | bytes 1179656 | tf_op jit(solution)/shard_map/ppermute | solution.py:1416
  244.4 20.7 %collective-permute-start.45 = (bf16[8,176,384]{2,1,0:T(8,128)(2,1)S(1)}, bf16[8,176,384]{2,1,0:T(8,128)(2,1)S(1)}, u32[]{:S(2)}, u32[]{:S(2)}) collective-permute-start(bf16[8,176,384]{2,1,0:T(8,128)(2,1)S(1)} %get-tuple-element.254), channel_id=1, source_target_pairs={{0,1},{1,0},{2,3},{3,2},{4,5},{5,4},{6,7},{7,6},{8,9},{9,8},{10,11... | collective-permute-start | bytes 3244040 | tf_op jit(solution)/shard_map/ppermute | solution.py:1416
  244.5 6.1 %collective-permute-start.38 = (bf16[128,768]{1,0:T(8,128)(2,1)S(1)}, bf16[128,768]{1,0:T(8,128)(2,1)S(1)}, u32[]{:S(2)}, u32[]{:S(2)}) collective-permute-start(bf16[128,768]{1,0:T(8,128)(2,1)S(1)} %collect.1.refs_7_), channel_id=1, source_target_pairs={{0,4},{4,0},{1,5},{5,1},{2,6},{6,2},{3,7},{7,3},{8,12},{12,8},{9,1... | collective-permute-start | bytes 589832 | tf_op jit(solution)/shard_map/ppermute | solution.py:1428
  244.8 22.4 %collective-permute-start.31 = (bf16[256,1536]{1,0:T(8,128)(2,1)S(1)}, bf16[256,1536]{1,0:T(8,128)(2,1)S(1)}, u32[]{:S(2)}, u32[]{:S(2)}) collective-permute-start(bf16[256,1536]{1,0:T(8,128)(2,1)S(1)} %get-tuple-element.239.refs_5_), channel_id=1, source_target_pairs={{0,1},{1,0},{2,3},{3,2},{4,5},{5,4},{6,7},{7,6},{8,9},{9,8},{10,11... | collective-permute-start | bytes 2359304 | tf_op jit(solution)/shard_map/ppermute | solution.py:1416
  250.6 10.1 %collective-permute-start.39 = (bf16[256,768]{1,0:T(8,128)(2,1)S(1)}, bf16[256,768]{1,0:T(8,128)(2,1)S(1)}, u32[]{:S(2)}, u32[]{:S(2)}) collective-permute-start(bf16[256,768]{1,0:T(8,128)(2,1)S(1)} %pad_maximum_fusion.2), channel_id=1, source_target_pairs={{0,8},{8,16},{16,24},{1,9},{9,17},{17,25},{2,10},{10,18},{18,26},{... | collective-permute-start | bytes 1179656 | tf_op jit(solution)/shard_map/ppermute | solution.py:1457
  253.6 18.8 %collective-permute-start.30 = (bf16[304,3840]{1,0:T(8,128)(2,1)}, bf16[304,3840]{1,0:T(8,128)(2,1)S(1)}, u32[]{:S(2)}, u32[]{:S(2)}) collective-permute-start(bf16[304,3840]{1,0:T(8,128)(2,1)} %get-tuple-element.237.refs_4_), channel_id=1, source_target_pairs={{0,1},{1,0},{2,3},{3,2},{4,5},{5,4},{6,7},{7,6},{8,9},{9,8},{10,11... | collective-permute-start | bytes 7004168 | tf_op jit(solution)/shard_map/ppermute | solution.py:1416
  255.2 25.9 %collective-permute-start.54 = (bf16[2,192,768]{2,1,0:T(8,128)(2,1)}, bf16[2,192,768]{2,1,0:T(8,128)(2,1)}, u32[]{:S(2)}, u32[]{:S(2)}) collective-permute-start(bf16[2,192,768]{2,1,0:T(8,128)(2,1)} %get-tuple-element.229.refs_3_), channel_id=1, source_target_pairs={{0,8},{8,0},{16,24},{24,16},{1,9},{9,1},{17,25},{25,17},{2,10},{10... | collective-permute-start | bytes 1769480 | tf_op jit(solution)/shard_map/ppermute | solution.py:1428
  260.7 28.6 %collective-permute-start.52 = (bf16[2,192,768]{2,1,0:T(8,128)(2,1)S(1)}, bf16[2,192,768]{2,1,0:T(8,128)(2,1)}, u32[]{:S(2)}, u32[]{:S(2)}) collective-permute-start(bf16[2,192,768]{2,1,0:T(8,128)(2,1)S(1)} %get-tuple-element.230.refs_2_.refs_4_), channel_id=1, source_target_pairs={{0,16},{8,24},{16,0},{24,8},{1,17},{9,25},{17,1},{25,9},{2,18},{10... | collective-permute-start | bytes 1769480 | tf_op jit(solution)/shard_map/ppermute | solution.py:1428
  267.0 23.9 %collective-permute-start.46 = (bf16[4,176,384]{2,1,0:T(8,128)(2,1)}, bf16[4,176,384]{2,1,0:T(8,128)(2,1)}, u32[]{:S(2)}, u32[]{:S(2)}) collective-permute-start(bf16[4,176,384]{2,1,0:T(8,128)(2,1)} %get-tuple-element.279), channel_id=1, source_target_pairs={{0,4},{4,0},{1,5},{5,1},{2,6},{6,2},{3,7},{7,3},{8,12},{12,8},{9,1... | collective-permute-start | bytes 1622024 | tf_op jit(solution)/shard_map/ppermute | solution.py:1428
  278.5 35.4 %collective-permute-start.32 = (bf16[4,48,2688]{2,1,0:T(8,128)(2,1)S(1)}, bf16[4,48,2688]{2,1,0:T(8,128)(2,1)S(1)}, u32[]{:S(2)}, u32[]{:S(2)}) collective-permute-start(bf16[4,48,2688]{2,1,0:T(8,128)(2,1)S(1)} %get-tuple-element.241), channel_id=1, source_target_pairs={{0,4},{4,0},{1,5},{5,1},{2,6},{6,2},{3,7},{7,3},{8,12},{12,8},{9,1... | collective-permute-start | bytes 3096584 | tf_op jit(solution)/shard_map/ppermute | solution.py:1428
  279.8 18.7 %collective-permute-start.42 = (bf16[256,768]{1,0:T(8,128)(2,1)S(1)}, bf16[256,768]{1,0:T(8,128)(2,1)S(1)}, u32[]{:S(2)}, u32[]{:S(2)}) collective-permute-start(bf16[256,768]{1,0:T(8,128)(2,1)S(1)} %copy-done.96), channel_id=1, source_target_pairs={{8,0},{16,8},{24,16},{9,1},{17,9},{25,17},{10,2},{18,10},{26,18},{... | collective-permute-start | bytes 1179656 | tf_op jit(solution)/shard_map/ppermute | solution.py:1458
  282.5 27.8 %collective-permute-start.55 = (bf16[1,192,768]{2,1,0:T(8,128)(2,1)S(1)}, bf16[1,192,768]{2,1,0:T(8,128)(2,1)S(1)}, u32[]{:S(2)}, u32[]{:S(2)}) collective-permute-start(bf16[1,192,768]{2,1,0:T(8,128)(2,1)S(1)} %get-tuple-element.267), channel_id=1, source_target_pairs={{0,16},{8,24},{16,0},{24,8},{1,17},{9,25},{17,1},{25,9},{2,18},{10... | collective-permute-start | bytes 884744 | tf_op jit(solution)/shard_map/ppermute | solution.py:1428
  290.6 21.8 %collective-permute-start.53 = (bf16[1,192,768]{2,1,0:T(8,128)(2,1)S(1)}, bf16[1,192,768]{2,1,0:T(8,128)(2,1)S(1)}, u32[]{:S(2)}, u32[]{:S(2)}) collective-permute-start(bf16[1,192,768]{2,1,0:T(8,128)(2,1)S(1)} %get-tuple-element.264), channel_id=1, source_target_pairs={{0,4},{4,0},{1,5},{5,1},{2,6},{6,2},{3,7},{7,3},{8,12},{12,8},{9,1... | collective-permute-start | bytes 884744 | tf_op jit(solution)/shard_map/ppermute | solution.py:1428
  292.1 19.6 %collective-permute-start.47 = (bf16[2,176,384]{2,1,0:T(8,128)(2,1)S(1)}, bf16[2,176,384]{2,1,0:T(8,128)(2,1)S(1)}, u32[]{:S(2)}, u32[]{:S(2)}) collective-permute-start(bf16[2,176,384]{2,1,0:T(8,128)(2,1)S(1)} %get-tuple-element.256), channel_id=1, source_target_pairs={{0,8},{8,0},{16,24},{24,16},{1,9},{9,1},{17,25},{25,17},{2,10},{10... | collective-permute-start | bytes 811016 | tf_op jit(solution)/shard_map/ppermute | solution.py:1428
  298.5 23.3 %collective-permute-start.40 = (bf16[256,768]{1,0:T(8,128)(2,1)S(1)}, bf16[256,768]{1,0:T(8,128)(2,1)}, u32[]{:S(2)}, u32[]{:S(2)}) collective-permute-start(bf16[256,768]{1,0:T(8,128)(2,1)S(1)} %copy-done.99), channel_id=1, source_target_pairs={{0,8},{8,16},{16,24},{1,9},{9,17},{17,25},{2,10},{10,18},{18,26},{... | collective-permute-start | bytes 1179656 | tf_op jit(solution)/shard_map/ppermute | solution.py:1457
  310.3 14.3 %collective-permute-start.43 = (bf16[256,768]{1,0:T(8,128)(2,1)S(1)}, bf16[256,768]{1,0:T(8,128)(2,1)}, u32[]{:S(2)}, u32[]{:S(2)}) collective-permute-start(bf16[256,768]{1,0:T(8,128)(2,1)S(1)} %collective-permute-done.42), channel_id=1, source_target_pairs={{8,0},{16,8},{24,16},{9,1},{17,9},{25,17},{10,2},{18,10},{26,18},{... | collective-permute-start | bytes 1179656 | tf_op jit(solution)/shard_map/ppermute | solution.py:1458
  312.3 9.4 %collective-permute-start.48 = (bf16[1,176,384]{2,1,0:T(8,128)(2,1)S(1)}, bf16[1,176,384]{2,1,0:T(8,128)(2,1)S(1)}, u32[]{:S(2)}, u32[]{:S(2)}) collective-permute-start(bf16[1,176,384]{2,1,0:T(8,128)(2,1)S(1)} %get-tuple-element.258), channel_id=1, source_target_pairs={{0,16},{8,24},{16,0},{24,8},{1,17},{9,25},{17,1},{25,9},{2,18},{10... | collective-permute-start | bytes 405512 | tf_op jit(solution)/shard_map/ppermute | solution.py:1428
  312.5 26.0 %copy-start.28 = (bf16[8,176,384]{2,1,0:T(8,128)(2,1)S(1)}, bf16[8,176,384]{2,1,0:T(8,128)(2,1)}, u32[]{:S(2)}) copy-start(bf16[8,176,384]{2,1,0:T(8,128)(2,1)} %copy-done.27) | copy-start | bytes 3244036
  312.5 25.9 %copy-start.9 = (bf16[8,128,768]{2,1,0:T(8,128)(2,1)S(1)}, bf16[8,128,768]{2,1,0:T(8,128)(2,1)}, u32[]{:S(2)}) copy-start(bf16[8,128,768]{2,1,0:T(8,128)(2,1)} %copy-done.8) | copy-start | bytes 4718596
  312.5 25.9 %copy-start.11 = (bf16[8,128,768]{2,1,0:T(8,128)(2,1)S(1)}, bf16[8,128,768]{2,1,0:T(8,128)(2,1)}, u32[]{:S(2)}) copy-start(bf16[8,128,768]{2,1,0:T(8,128)(2,1)} %copy-done.10) | copy-start | bytes 4718596
  312.6 25.9 %copy-start.79 = (s32[4]{0:T(128)S(1)}, s32[4]{0:T(128)}, u32[]{:S(2)}) copy-start(s32[4]{0:T(128)} %copy-done.78) | copy-start | bytes 52
  312.6 55.5 %collective-permute-start.56 = (bf16[384,768]{1,0:T(8,128)(2,1)S(1)}, bf16[384,768]{1,0:T(8,128)(2,1)S(1)}, u32[]{:S(2)}, u32[]{:S(2)}) collective-permute-start(bf16[384,768]{1,0:T(8,128)(2,1)S(1)} %pad_maximum_fusion.refs_2_), channel_id=1, source_target_pairs={{0,2},{2,0},{1,3},{3,1},{4,6},{6,4},{5,7},{7,5},{8,10},{10,8},{9,1... | collective-permute-start | bytes 1769480 | tf_op jit(solution)/shard_map/ppermute | solution.py:1420
  314.6 22.4 %collective-permute-start.33 = (bf16[2,48,2688]{2,1,0:T(8,128)(2,1)S(1)}, bf16[2,48,2688]{2,1,0:T(8,128)(2,1)S(1)}, u32[]{:S(2)}, u32[]{:S(2)}) collective-permute-start(bf16[2,48,2688]{2,1,0:T(8,128)(2,1)S(1)} %get-tuple-element.243), channel_id=1, source_target_pairs={{0,8},{8,0},{16,24},{24,16},{1,9},{9,1},{17,25},{25,17},{2,10},{10... | collective-permute-start | bytes 1548296 | tf_op jit(solution)/shard_map/ppermute | solution.py:1428
  321.7 9.6 %collective-permute-start.49 = (bf16[1,176,384]{2,1,0:T(8,128)(2,1)S(1)}, bf16[1,176,384]{2,1,0:T(8,128)(2,1)S(1)}, u32[]{:S(2)}, u32[]{:S(2)}) collective-permute-start(bf16[1,176,384]{2,1,0:T(8,128)(2,1)S(1)} %add_convert_fusion.6), channel_id=1, source_target_pairs={{0,16},{8,24},{16,0},{24,8},{1,17},{9,25},{17,1},{25,9},{2,18},{10... | collective-permute-start | bytes 405512 | tf_op jit(solution)/shard_map/ppermute | solution.py:1428
  321.8 23.9 %collective-permute-start.41 = (bf16[256,768]{1,0:T(8,128)(2,1)}, bf16[256,768]{1,0:T(8,128)(2,1)}, u32[]{:S(2)}, u32[]{:S(2)}) collective-permute-start(bf16[256,768]{1,0:T(8,128)(2,1)} %collective-permute-done.40), channel_id=1, source_target_pairs={{0,8},{8,16},{16,24},{1,9},{9,17},{17,25},{2,10},{10,18},{18,26},{... | collective-permute-start | bytes 1179656 | tf_op jit(solution)/shard_map/ppermute | solution.py:1457
  324.6 29.0 %collective-permute-start.44 = (bf16[256,768]{1,0:T(8,128)(2,1)}, bf16[256,768]{1,0:T(8,128)(2,1)}, u32[]{:S(2)}, u32[]{:S(2)}) collective-permute-start(bf16[256,768]{1,0:T(8,128)(2,1)} %collective-permute-done.43), channel_id=1, source_target_pairs={{8,0},{16,8},{24,16},{9,1},{17,9},{25,17},{10,2},{18,10},{26,18},{... | collective-permute-start | bytes 1179656 | tf_op jit(solution)/shard_map/ppermute | solution.py:1458
  332.1 36.1 %collective-permute-start.50 = (bf16[2,176,384]{2,1,0:T(8,128)(2,1)}, bf16[2,176,384]{2,1,0:T(8,128)(2,1)}, u32[]{:S(2)}, u32[]{:S(2)}) collective-permute-start(bf16[2,176,384]{2,1,0:T(8,128)(2,1)} %pad_maximum_fusion.4), channel_id=1, source_target_pairs={{0,8},{8,0},{16,24},{24,16},{1,9},{9,1},{17,25},{25,17},{2,10},{10... | collective-permute-start | bytes 811016 | tf_op jit(solution)/shard_map/ppermute | solution.py:1428
  337.7 31.9 %collective-permute-start.34 = (bf16[1,48,2688]{2,1,0:T(8,128)(2,1)S(1)}, bf16[1,48,2688]{2,1,0:T(8,128)(2,1)}, u32[]{:S(2)}, u32[]{:S(2)}) collective-permute-start(bf16[1,48,2688]{2,1,0:T(8,128)(2,1)S(1)} %get-tuple-element.245), channel_id=1, source_target_pairs={{0,16},{8,24},{16,0},{24,8},{1,17},{9,25},{17,1},{25,9},{2,18},{10... | collective-permute-start | bytes 774152 | tf_op jit(solution)/shard_map/ppermute | solution.py:1428
  345.7 26.2 %collective-permute-start.29 = (bf16[8,32,1408]{2,1,0:T(8,128)(2,1)}, bf16[8,32,1408]{2,1,0:T(8,128)(2,1)}, u32[]{:S(2)}, u32[]{:S(2)}) collective-permute-start(bf16[8,32,1408]{2,1,0:T(8,128)(2,1)} %get-tuple-element.234), channel_id=1, source_target_pairs={{0,1},{1,0},{2,3},{3,2},{4,5},{5,4},{6,7},{7,6},{8,9},{9,8},{10,11... | collective-permute-start | bytes 2162696 | tf_op jit(solution)/shard_map/ppermute | solution.py:1416
  364.2 19.0 %collective-permute-start.57 = (bf16[384,768]{1,0:T(8,128)(2,1)S(1)}, bf16[384,768]{1,0:T(8,128)(2,1)S(1)}, u32[]{:S(2)}, u32[]{:S(2)}) collective-permute-start(bf16[384,768]{1,0:T(8,128)(2,1)S(1)} %pad_maximum_fusion.refs_2_), channel_id=1, source_target_pairs={{0,1},{1,0},{2,3},{3,2},{4,5},{5,4},{6,7},{7,6},{8,9},{9,8},{10,11... | collective-permute-start | bytes 1769480 | tf_op jit(solution)/shard_map/ppermute | solution.py:1416
  368.1 15.1 %collective-permute-start.58 = (bf16[384,768]{1,0:T(8,128)(2,1)S(1)}, bf16[384,768]{1,0:T(8,128)(2,1)S(1)}, u32[]{:S(2)}, u32[]{:S(2)}) collective-permute-start(bf16[384,768]{1,0:T(8,128)(2,1)S(1)} %collective-permute-done.56.refs_3_), channel_id=1, source_target_pairs={{0,1},{1,0},{2,3},{3,2},{4,5},{5,4},{6,7},{7,6},{8,9},{9,8},{10,11... | collective-permute-start | bytes 1769480 | tf_op jit(solution)/shard_map/ppermute | solution.py:1416
  369.3 16.9 %collective-permute-start.51 = (bf16[4,176,384]{2,1,0:T(8,128)(2,1)S(1)}, bf16[4,176,384]{2,1,0:T(8,128)(2,1)}, u32[]{:S(2)}, u32[]{:S(2)}) collective-permute-start(bf16[4,176,384]{2,1,0:T(8,128)(2,1)S(1)} %pad_maximum_fusion.1.refs_1_), channel_id=1, source_target_pairs={{0,4},{4,0},{1,5},{5,1},{2,6},{6,2},{3,7},{7,3},{8,12},{12,8},{9,1... | collective-permute-start | bytes 1622024 | tf_op jit(solution)/shard_map/ppermute | solution.py:1428
  370.7 7.2 %collective-permute-start.35 = (bf16[48,2688]{1,0:T(8,128)(2,1)S(1)}, bf16[48,2688]{1,0:T(8,128)(2,1)S(1)}, u32[]{:S(2)}, u32[]{:S(2)}) collective-permute-start(bf16[48,2688]{1,0:T(8,128)(2,1)S(1)} %fusion.14.refs_2_), channel_id=1, source_target_pairs={{0,2},{2,0},{1,3},{3,1},{4,6},{6,4},{5,7},{7,5},{8,10},{10,8},{9,1... | collective-permute-start | bytes 774152 | tf_op jit(solution)/shard_map/ppermute | solution.py:1420
  371.9 17.0 %collective-permute-start.36 = (bf16[48,2688]{1,0:T(8,128)(2,1)S(1)}, bf16[48,2688]{1,0:T(8,128)(2,1)}, u32[]{:S(2)}, u32[]{:S(2)}) collective-permute-start(bf16[48,2688]{1,0:T(8,128)(2,1)S(1)} %fusion.14.refs_2_), channel_id=1, source_target_pairs={{0,1},{1,0},{2,3},{3,2},{4,5},{5,4},{6,7},{7,6},{8,9},{9,8},{10,11... | collective-permute-start | bytes 774152 | tf_op jit(solution)/shard_map/ppermute | solution.py:1416
  377.9 11.0 %collective-permute-start.37 = (bf16[48,2688]{1,0:T(8,128)(2,1)S(1)}, bf16[48,2688]{1,0:T(8,128)(2,1)}, u32[]{:S(2)}, u32[]{:S(2)}) collective-permute-start(bf16[48,2688]{1,0:T(8,128)(2,1)S(1)} %collective-permute-done.35.refs_3_), channel_id=1, source_target_pairs={{0,1},{1,0},{2,3},{3,2},{4,5},{5,4},{6,7},{7,6},{8,9},{9,8},{10,11... | collective-permute-start | bytes 774152 | tf_op jit(solution)/shard_map/ppermute | solution.py:1416
  (117 other events, 727.6 us)
where the time goes:
time: 399 us; the launch traced here: 392 us
  Pallas kernels  178 us (45%)
  starting transfers between devices  85.2 us (21%)
  waiting for transfers between devices  60.1 us (15%)
  local copies, waits for them, and re-layouts  52.6 us (13%)
  other arithmetic  12.5 us (3%)
    pallas_call x35, Pallas kernels, call(): pl.pallas_call(body, grid=grid, in_specs=in_specs + [pl.BlockSpec(memory_...  150 us
    unnamed x250, local copies, waits for them, and re-layouts  43.1 us
    ppermute x20, starting transfers between devices, exchange(): return lax.ppermute(values, axis, [(s, s ^ bit) for s in range(size)])  29.9 us
    ppermute x23, starting transfers between devices, swap_core(): return lax.ppermute(values, 'core', [(0, 1), (1, 0)])  29.4 us
    pallas_call x2, Pallas kernels, ff_backward(): pl.pallas_call(body, grid_spec=gs, out_shape=[jax.ShapeDtypeStruct((count...  28.3 us
    ppermute x20, waiting for transfers between devices, exchange(): return lax.ppermute(values, axis, [(s, s ^ bit) for s in range(size)])  27.7 us
    ppermute x7, waiting for transfers between devices, from_x(): lax.ppermute(values, 'x', [(s, (s - step) % size) for s in range(size)])  21.9 us
    ppermute x3, starting transfers between devices, pass_on(): rising.append(lax.ppermute(rising[-1], axis, up))  14.2 us
  transfers between devices with their start and end apart: 56, of which 16 were waited for; matrix products, arithmetic and copies ran while one was open for 4% of the time, Pallas kernels for 35%

commit v1 on v0

--- a/solution.py
+++ b/solution.py
@@ -174,6 +174,9 @@
     if not grid:
         held = sum(math.prod(v.shape) * jnp.dtype(v.dtype).itemsize for v in scratch)
         limit = min(VMEM_BYTES, moved + held + VMEM_SPARE)
+    elif grid == (1,):
+        held = sum(math.prod(v.shape) * jnp.dtype(v.dtype).itemsize for v in scratch)
+        limit = min(VMEM_BYTES, 2 * moved + held + VMEM_SPARE)
     count = len(ins)
 
     def body(*refs):
@@ -349,6 +352,7 @@
         ],
         flops=2 * items * rows * width * width * 6,
         name="self_forward",
+        grid=(1,),
     )
 
 
@@ -671,13 +675,22 @@
 
 
 def contrast_kernel(
-    queries, slots, info, gathered, sharpness, loss, grad_image, grad_text, grad_sharp,
-    all_loss, all_image, all_text,
+    queries, slots, y_size, z_size, info, sharpness, *rest
 ):
+    pieces = rest[:z_size]
+    (
+        loss, grad_image, grad_text, grad_sharp, all_ids, gathered, all_loss, all_image, all_text
+    ) = rest[z_size:]
+    each = pieces[0].shape[0] // y_size
+    for k, piece in enumerate(pieces):
+        for j in range(y_size):
+            at = pl.multiple_of((info[DP] ^ (k * y_size + j)) * each, 8)
+            gathered[pl.ds(at, each), :] = piece[j * each : (j + 1) * each]
     count = gathered.shape[0]
     emb = grad_image.shape[1]
     image_raw, text_raw = gathered[:, :emb], gathered[:, emb : 2 * emb]
     ids = gathered[:, 2 * emb :]
+    all_ids[...] = ids.astype(jnp.int32)
     pairs = ids[:, slots : slots + 1].astype(jnp.int32)
     pairs_row = ids.T[slots : slots + 1].astype(jnp.int32)
     image_scale = lax.rsqrt(jnp.sum(image_raw * image_raw, axis=1, keepdims=True) + 1e-06)
@@ -720,13 +733,21 @@
     grad_text[...] = jnp.concatenate([all_text[mine, :], all_text[theirs, :]], axis=0).astype(BF)
 
 
-def contrast(info, gathered, sharpness, queries, slots, group, emb, after):
-    count = gathered.shape[0]
-    return call(
-        functools.partial(contrast_kernel, queries, slots),
-        [info, gathered, sharpness],
-        [((group, 1), F32), ((group, emb), BF), ((group, emb), BF), ((1, 1), F32)],
+def contrast(info, pieces, sharpness, queries, slots, group, emb, y_size, after):
+    count = pieces[0].shape[0] * len(pieces)
+    spare = pieces[0].shape[1] - 2 * emb
+    return call(
+        functools.partial(contrast_kernel, queries, slots, y_size, len(pieces)),
+        [info, sharpness, *pieces],
+        [
+            ((group, 1), F32),
+            ((group, emb), BF),
+            ((group, emb), BF),
+            ((1, 1), F32),
+            ((count, spare), jnp.int32),
+        ],
         scratch=[
+            pltpu.VMEM((count, pieces[0].shape[1]), F32),
             pltpu.VMEM((count, 1), F32),
             pltpu.VMEM((count, emb), F32),
             pltpu.VMEM((count, emb), F32),
@@ -789,6 +810,7 @@
         scratch=[pltpu.VMEM((count, width), BF)],
         flops=4 * count * width * width + 8 * count * all_rows * width,
         name="cross_backward",
+        grid=(1,),
         after=after,
     )
 
@@ -1628,12 +1650,14 @@
     gathered = gather_doubling(
         jnp.concatenate([image_raw, text_raw, own_ids], axis=1), "core", CORES
     )
-    gathered = gather_doubling(gather_doubling(gathered, "y", y_size), "z", z_size)
-    loss, grad_image, grad_text, grad_sharp = contrast(
-        info, gathered, sharpness.reshape(1, 1), queries, slots, group, emb, [hidden_out]
-    )
-    ids = gathered[:, 2 * emb : 2 * emb + slots].astype(jnp.int32)
-    all_tokens = ids.reshape(dp_size, group * slots)
+    gathered = jnp.concatenate(
+        [gathered] + [exchange(gathered, "y", y_size, j) for j in range(1, y_size)], axis=0
+    )
+    pieces = [gathered] + [exchange(gathered, "z", z_size, k) for k in range(1, z_size)]
+    loss, grad_image, grad_text, grad_sharp, ids = contrast(
+        info, pieces, sharpness.reshape(1, 1), queries, slots, group, emb, y_size, [hidden_out]
+    )
+    all_tokens = ids[:, :slots].reshape(dp_size, group * slots)
 
     q_rhs, grad_second, q_vectors = ff_backward(
         info, incoming, 0, grad_image, (q_slope, q_normal, q_scale),

time: 399 us -> 394 us (0.987)
  starting transfers between devices: 85.2 us -> 97.6 us
  Pallas kernels: 178 us -> 172 us
  waiting for transfers between devices: 60.1 us -> 56 us
  other arithmetic: 12.5 us -> 8.43 us
    ppermute x3, starting transfers between devices: 14.2 us -> 21.5 us  [pass_on(): rising.append(lax.ppermute(rising[-1], axis, up))]
    pallas_call x35, Pallas kernels: 150 us -> 144 us  [call(): pl.pallas_call(body, grid=grid, in_specs=in_specs + [pl.BlockSpec(memory_...]
    ppermute x3, waiting for transfers between devices: 5.69 us -> 0.01 us  [pass_on(): falling.append(lax.ppermute(falling[-1], axis, down))]
    ppermute x20 -> x21, starting transfers between devices: 29.9 us -> 34.9 us  [exchange(): return lax.ppermute(values, axis, [(s, s ^ bit) for s in range(size)])]
    ppermute x20 -> x21, waiting for transfers between devices: 27.7 us -> 31 us  [exchange(): return lax.ppermute(values, axis, [(s, s ^ bit) for s in range(size)])]
    unnamed x250 -> x218, local copies, waits for them, and re-layouts: 43.1 us -> 40 us
  transfers between devices with their start and end apart: 56 -> 57, of which waited for: 16 -> 16; matrix products, arithmetic and copies ran while one was open for 4% -> 4% of each run, Pallas kernels for 35% -> 34%
where the time goes in v1:
time: 394 us; the launch traced here: 388 us
  Pallas kernels  172 us (44%)
  starting transfers between devices  97.6 us (25%)
  waiting for transfers between devices  56 us (14%)
  local copies, waits for them, and re-layouts  50.3 us (13%)
  other arithmetic  8.43 us (2%)
    pallas_call x35, Pallas kernels, call(): pl.pallas_call(body, grid=grid, in_specs=in_specs + [pl.BlockSpec(memory_...  144 us
    unnamed x218, local copies, waits for them, and re-layouts  40 us
    ppermute x21, starting transfers between devices, exchange(): return lax.ppermute(values, axis, [(s, s ^ bit) for s in range(size)])  34.9 us
    ppermute x21, waiting for transfers between devices, exchange(): return lax.ppermute(values, axis, [(s, s ^ bit) for s in range(size)])  31 us
    ppermute x23, starting transfers between devices, swap_core(): return lax.ppermute(values, 'core', [(0, 1), (1, 0)])  29.4 us
    pallas_call x2, Pallas kernels, ff_backward(): pl.pallas_call(body, grid_spec=gs, out_shape=[jax.ShapeDtypeStruct((count...  28.3 us
    ppermute x3, starting transfers between devices, pass_on(): rising.append(lax.ppermute(rising[-1], axis, up))  21.5 us
    ppermute x7, waiting for transfers between devices, from_x(): lax.ppermute(values, 'x', [(s, (s - step) % size) for s in range(size)])  20.1 us
  transfers between devices with their start and end apart: 57, of which 16 were waited for; matrix products, arithmetic and copies ran while one was open for 4% of the time, Pallas kernels for 34%

profile of v1, /device:TPU:1, one launch (start us, length us, event | category | flops | bytes accessed | tf_op | source)
XLA Modules:
  0.0 387.9 jit_solution(4781238469877307020)
XLA Ops:
  0.7 2.5 constant_dynamic-slice_fusion.1
  6.1 8.4 %words.1 = (bf16[256,768]{1,0:T(8,128)(2,1)}, bf16[256,768]{1,0:T(8,128)(2,1)}) custom-call(s32[6]{0:T(128)S(1)} %stack.36.refs_0_, s32[512,1]{1,0:T(8,128)} %sub.36.refs_1_, bf16[3840,768]{1,0:T(8,128)(2,1)} %refs_2_.5), custom_call_target="tpu_custom_call" | custom-call | flops 1 | bytes 1 | tf_op jit(solution)/shard_map/words/pallas_call | solution.py:185
  15.0 1.6 collective-permute-done.3
  17.7 2.6 collective-permute-start.4
  20.3 2.7 stage.3
  26.3 3.4 collective-permute-done.4.refs_12_.refs_17_
  41.2 8.7 %self_forward.1 = (bf16[512,2304]{1,0:T(8,128)(2,1)S(1)}, bf16[12,512,128]{2,1,0:T(8,128)(2,1)S(1)}, f32[256,768]{1,0:T(8,128)S(1)}, f32[256,768]{1,0:T(8,128)S(...) custom-call(s32[6]{0:T(128)} %copy-done.96, ...), custom_call_target="tpu_custom_call" | custom-call | flops 1 | bytes 1 | tf_op jit(solution)/shard_map/self_forward/pallas_call | solution.py:185
  51.2 1.9 collective-permute-start.12
  53.1 2.3 stage.4
  60.6 11.4 %ff_forward.2 = (bf16[256,3072]{1,0:T(8,128)(2,1)}, bf16[960,256]{1,0:T(8,128)(2,1)}, bf16[960,256]{1,0:T(8,128)(2,1)}, f32[256,768]{1,0:T(8,128)}, f32[256,1]{1...) custom-call(s32[6]{0:T(128)S(1)} %copy-done.98, f32[256,768]{1,0:T(8,128)} %copy-done.28, f32[768]{0:T(1024)} %refs_7_.9, ...), custom_call_target="tpu_custom_call" | custom-call | flops 1 | bytes 1 | tf_op jit(solution)/shard_map/ff_forward/pallas_call | solution.py:185
  72.1 11.8 %collective-permute-done.7.refs_5_.refs_6_ = bf16[8,32,1408]{2,1,0:T(8,128)(2,1)} collective-permute-done((bf16[8,32,1408]{2,1,0:T(8,128)(2,1)}, bf16[8,32,1408]{2,1,0:T(8,128)(2,1)}, u32[]{:S(2)}, u32[]{:S(2)}) %collective-permute-start.7) | collective-permute-done | bytes 720928 | tf_op jit(solution)/shard_map/ppermute | solution.py:1442
  85.0 8.4 %key_value.1 = (bf16[8,128,768]{2,1,0:T(8,128)(2,1)S(1)}, bf16[8,128,768]{2,1,0:T(8,128)(2,1)S(1)}) custom-call(s32[6]{0:T(128)S(1)} %copy-done.98, s32[4]{0:T(128)S(1)} %pad_add_fusion.refs_1_, bf16[8,32,1408]{2,1,0:T(8,128)(2,1)} %get-tuple-element.280.refs_2_.refs_3_, bf16[8,32,1408]{2,1,0:T(8,128)(2,1)} %collective-permute-done.5.refs_1_.refs_3_.refs_4_, ...), custom_call_target="tpu_custom_call" | custom-call | flops 1 | bytes 1 | tf_op jit(solution)/shard_map/key_value/pallas_call | solution.py:185
  93.6 3.4 cross_forward.1
  100.7 11.2 %ff_forward.3 = (bf16[256,3072]{1,0:T(8,128)(2,1)}, bf16[960,256]{1,0:T(8,128)(2,1)}, bf16[960,256]{1,0:T(8,128)(2,1)}, f32[256,768]{1,0:T(8,128)}, f32[256,1]{1...) custom-call(s32[6]{0:T(128)S(1)} %copy-done.98, f32[256,768]{1,0:T(8,128)} %copy-done.30, f32[768]{0:T(1024)} %refs_4_.8, ...), custom_call_target="tpu_custom_call" | custom-call | flops 1 | bytes 1 | tf_op jit(solution)/shard_map/ff_forward/pallas_call | solution.py:185
  115.9 1.6 collective-permute-start.17
  120.9 1.5 collective-permute-start.18
  122.5 2.9 collective-permute-done.18.refs_3_
  126.0 2.4 collective-permute-start.19
  128.4 2.0 collective-permute-done.19.refs_4_
  131.1 3.5 collective-permute-start.24
  134.6 3.1 collective-permute-start.20
  138.3 2.6 hidden_assemble.1.refs_6_
  142.4 2.3 contrast.1
  147.2 9.9 %ff_backward.2 = (bf16[256,3840]{1,0:T(8,128)(2,1)}, f32[256,768]{1,0:T(8,128)}, f32[2,768]{1,0:T(2,128)}) custom-call(s32[6]{0:T(128)S(1)} %copy-done.98, bf16[16,64,768]{2,1,0:T(8,128)(2,1)} %refs_1_.5, bf16[16,256]{1,0:T(8,128)(2,1)} %copy-done.85, bf16[768,256]{1,0:T(8,128)(2,1)} %refs_3_.10, f32[256,768]{1,0:T(8,128)} %get-tuple-element.198.refs_4_, ...), custom_call_target="tpu_custom_call" | custom-call | flops 1 | bytes 1 | tf_op jit(solution)/shard_map/ff_backward/pallas_call | solution.py:623
  157.7 18.3 %ff_backward.3 = (bf16[256,3840]{1,0:T(8,128)(2,1)}, f32[256,768]{1,0:T(8,128)}, f32[2,768]{1,0:T(2,128)}) custom-call(s32[6]{0:T(128)S(1)} %copy-done.98, bf16[16,64,768]{2,1,0:T(8,128)(2,1)} %refs_1_.5, bf16[16,256]{1,0:T(8,128)(2,1)} %copy-done.81, bf16[768,256]{1,0:T(8,128)(2,1)} %refs_3_.11, f32[256,768]{1,0:T(8,128)} %get-tuple-element.187.refs_14_.refs_4_, ...), custom_call_target="tpu_custom_call" | custom-call | flops 1 | bytes 1 | tf_op jit(solution)/shard_map/ff_backward/pallas_call | solution.py:623
  176.2 1.5 copy-done.32
  178.4 4.3 %ff_weights.2 = (bf16[4,192,768]{2,1,0:T(8,128)(2,1)S(1)}, bf16[4,192,768]{2,1,0:T(8,128)(2,1)}) custom-call(s32[6]{0:T(128)S(1)} %copy-done.98, bf16[960,256]{1,0:T(8,128)(2,1)S(1)} %copy-done.48, bf16[960,256]{1,0:T(8,128)(2,1)} %collective-permute-done.22.refs_11_.refs_2_, bf16[256,3840]{1,0:T(8,128)(2,1)S(1)} %copy-done.32, ...), custom_call_target="tpu_custom_call" | custom-call | flops 1 | bytes 1 | tf_op jit(solution)/shard_map/ff_weights/pallas_call | solution.py:185
  182.7 3.9 %ff_weights.3 = (bf16[4,192,768]{2,1,0:T(8,128)(2,1)S(1)}, bf16[4,192,768]{2,1,0:T(8,128)(2,1)}) custom-call(s32[6]{0:T(128)S(1)} %copy-done.98, bf16[960,256]{1,0:T(8,128)(2,1)S(1)} %copy-done.47, bf16[960,256]{1,0:T(8,128)(2,1)} %collective-permute-done.21.refs_12_.refs_2_, bf16[256,3840]{1,0:T(8,128)(2,1)S(1)} %copy-done.33, ...), custom_call_target="tpu_custom_call" | custom-call | flops 1 | bytes 1 | tf_op jit(solution)/shard_map/ff_weights/pallas_call | solution.py:185
  188.9 1.5 reshape.100.refs_1_
  202.5 9.1 %cross_backward.1 = (bf16[256,1536]{1,0:T(8,128)(2,1)S(1)}, bf16[8,128,768]{2,1,0:T(8,128)(2,1)S(1)}, bf16[8,128,768]{2,1,0:T(8,128)(2,1)S(1)}, f32[256,768]{1,0:T(8,128)S(1)}, f32[2,768]{1,0:T(2,128)S(1)}) custom-call(s32[6]{0:T(128)S(1)} %copy-done.98, f32[256,768]{1,0:T(8,128)S(1)} %copy-done.45, f32[256,768]{1,0:T(8,128)S(1)} %copy-done.31, ...), custom_call_target="tpu_custom_call" | custom-call | flops 1 | bytes 1 | tf_op jit(solution)/shard_map/cross_backward/pallas_call | solution.py:185
  211.8 9.5 %self_backward.1 = (bf16[304,3840]{1,0:T(8,128)(2,1)S(1)}, bf16[256,768]{1,0:T(8,128)(2,1)S(1)}) custom-call(s32[6]{0:T(128)S(1)} %copy-done.98, f32[256,768]{1,0:T(8,128)S(1)} %get-tuple-element.222.refs_1_, f32[256,768]{1,0:T(8,128)S(1)} %copy-done.46, f32[256,768]{1,0:T(8,128)S(1)} %copy-done.27, f32[256,768]{1,0:T(8,128)S(1)} %copy-done.29, ...), custom_call_target="tpu_custom_call" | custom-call | flops 1 | bytes 1 | tf_op jit(solution)/shard_map/self_backward/pallas_call | solution.py:185
  221.3 1.6 halve.8
  223.0 1.6 halve.9
  226.0 5.3 %slots.1 = (s32[8,512]{1,0:T(8,128)S(1)}, s32[1,1024]{1,0:T(1,128)S(1)}, s32[1,1]{1,0:T(1,128)}) custom-call(s32[6]{0:T(128)S(1)} %copy-done.98, s32[8,512]{1,0:T(8,128)S(1)} %copy-done.106, bf16[256,768]{1,0:T(8,128)(2,1)S(1)} %stage.5.refs_2_), custom_call_target="tpu_custom_call" | custom-call | flops 99999997952 | bytes 1 | tf_op jit(solution)/shard_map/slots/pallas_call | solution.py:185
  232.0 8.0 %kv_weights.1 = (bf16[8,176,384]{2,1,0:T(8,128)(2,1)S(1)}, bf16[8,176,384]{2,1,0:T(8,128)(2,1)S(1)}) custom-call(s32[6]{0:T(128)S(1)} %copy-done.98, bf16[8,128,768]{2,1,0:T(8,128)(2,1)S(1)} %get-tuple-element.219.refs_1_.refs_2_, bf16[8,128,768]{2,1,0:T(8,128)(2,1)S(1)} %get-tuple-element.220.refs_2_.refs_3_, ...), custom_call_target="tpu_custom_call" | custom-call | flops 1 | bytes 1 | tf_op jit(solution)/shard_map/kv_weights/pallas_call | solution.py:185
  241.1 5.1 %collective-permute-done.39 = bf16[128,768]{1,0:T(8,128)(2,1)S(1)} collective-permute-done((bf16[128,768]{1,0:T(8,128)(2,1)S(1)}, bf16[128,768]{1,0:T(8,128)(2,1)S(1)}, u32[]{:S(2)}, u32[]{:S(2)}) %collective-permute-start.39) | collective-permute-done | bytes 196640 | tf_op jit(solution)/shard_map/ppermute | solution.py:1450
  246.3 3.7 collective-permute-start.40
  250.0 1.6 collective-permute-start.31
  251.6 2.1 collective-permute-start.55
  253.7 3.3 collective-permute-done.40.refs_3_
  257.1 4.1 %collective-permute-start.53 = (bf16[2,192,768]{2,1,0:T(8,128)(2,1)S(1)}, bf16[2,192,768]{2,1,0:T(8,128)(2,1)S(1)}, u32[]{:S(2)}, u32[]{:S(2)}) collective-permute-start(bf16[2,192,768]{2,1,0:T(8,128)(2,1)S(1)} %get-tuple-element.232.refs_2_.refs_4_), channel_id=1, source_target_pairs={{0,16},{8,24},{16,0},{24,8},{1,17},{9,25},{17,1},{25,9},{2,18},{10... | collective-permute-start | bytes 1769480 | tf_op jit(solution)/shard_map/ppermute | solution.py:1450
  263.2 2.7 mid_weights.1.refs_6_
  265.9 2.4 last_weights.1
  270.1 3.1 collective-permute-done.55.refs_2_
  273.9 9.5 %collective-permute-start.56 = (bf16[1,192,768]{2,1,0:T(8,128)(2,1)S(1)}, bf16[1,192,768]{2,1,0:T(8,128)(2,1)S(1)}, u32[]{:S(2)}, u32[]{:S(2)}) collective-permute-start(bf16[1,192,768]{2,1,0:T(8,128)(2,1)S(1)} %get-tuple-element.269), channel_id=1, source_target_pairs={{0,16},{8,24},{16,0},{24,8},{1,17},{9,25},{17,1},{25,9},{2,18},{10... | collective-permute-start | bytes 884744 | tf_op jit(solution)/shard_map/ppermute | solution.py:1450
  283.4 1.6 collective-permute-done.53.refs_2_
  287.3 15.3 %collective-permute-start.41 = (bf16[256,768]{1,0:T(8,128)(2,1)S(1)}, bf16[256,768]{1,0:T(8,128)(2,1)}, u32[]{:S(2)}, u32[]{:S(2)}) collective-permute-start(bf16[256,768]{1,0:T(8,128)(2,1)S(1)} %collective-permute-done.40.refs_3_), channel_id=1, source_target_pairs={{0,8},{8,16},{16,24},{1,9},{9,17},{17,25},{2,10},{10,18},{18,26},{... | collective-permute-start | bytes 1179656 | tf_op jit(solution)/shard_map/ppermute | solution.py:1479
  302.6 3.4 collective-permute-done.56
  310.3 2.2 collective-permute-start.34
  312.5 5.0 %collective-permute-done.49 = bf16[1,176,384]{2,1,0:T(8,128)(2,1)S(1)} collective-permute-done((bf16[1,176,384]{2,1,0:T(8,128)(2,1)S(1)}, bf16[1,176,384]{2,1,0:T(8,128)(2,1)S(1)}, u32[]{:S(2)}, u32[]{:S(2)}) %collective-permute-start.49) | collective-permute-done | bytes 135200 | tf_op jit(solution)/shard_map/ppermute | solution.py:1450
  317.6 2.6 collective-permute-start.42
  321.5 5.6 %collective-permute-done.50 = bf16[1,176,384]{2,1,0:T(8,128)(2,1)S(1)} collective-permute-done((bf16[1,176,384]{2,1,0:T(8,128)(2,1)S(1)}, bf16[1,176,384]{2,1,0:T(8,128)(2,1)S(1)}, u32[]{:S(2)}, u32[]{:S(2)}) %collective-permute-start.50) | collective-permute-done | bytes 135200 | tf_op jit(solution)/shard_map/ppermute | solution.py:1450
  327.8 3.8 collective-permute-start.51
  333.7 6.0 %features_back.1 = (f32[8,32,1408]{2,1,0:T(8,128)S(1)}, bf16[8,32,1408]{2,1,0:T(8,128)(2,1)}) custom-call(s32[6]{0:T(128)S(1)} %copy-done.98, s32[4]{0:T(128)S(1)} %copy-done.79, bf16[8,128,768]{2,1,0:T(8,128)(2,1)S(1)} %get-tuple-element.219.refs_1_.refs_2_, bf16[8,128,768]{2,1,0:T(8,128)(2,1)S(1)} %get-tuple-element.220.refs_2_.refs_3_, ...), custom_call_target="tpu_custom_call" | custom-call | flops 1 | bytes 1 | tf_op jit(solution)/shard_map/features_back/pallas_call | solution.py:185
  340.8 9.4 %collective-permute-start.30 = (bf16[8,32,1408]{2,1,0:T(8,128)(2,1)}, bf16[8,32,1408]{2,1,0:T(8,128)(2,1)}, u32[]{:S(2)}, u32[]{:S(2)}) collective-permute-start(bf16[8,32,1408]{2,1,0:T(8,128)(2,1)} %get-tuple-element.236), channel_id=1, source_target_pairs={{0,1},{1,0},{2,3},{3,2},{4,5},{5,4},{6,7},{7,6},{8,9},{9,8},{10,11... | collective-permute-start | bytes 2162696 | tf_op jit(solution)/shard_map/ppermute | solution.py:1438
  350.2 10.5 %conditional.1 = (f32[3840,768]{1,0:T(8,128)}) conditional(s32[]{:T(128)} %bitcast.12, (s32[]{:T(128)}, s32[8,512]{1,0:T(8,128)S(1)}, s32[]{:T(128)}, s32[]{:T(128)}, bf16[256,768]{1,0:T(8,128)(2,1)S(1)}, /*index=5*/bf16[256,768]{1,0:T(8,128)(2,1)S(1)}) %tuple.37, (s32[6]{0:T(128)S(1)}, s32[1,1024]{1,0:T(1,128)S(1)}, bf16[256,768]{1,0:T(8,128)(2,1)S(1)}, ...), branch_computations={%region_0.1_spmd, %region_1.2_spmd} | conditional | flops 3065122560 | bytes 161648864 | solution.py:1719
  350.4 10.3 %table.1 = f32[3840,768]{1,0:T(8,128)} custom-call(s32[6]{0:T(128)S(1)} %get-tuple-element.39.refs_0_, s32[1,1024]{1,0:T(1,128)S(1)} %get-tuple-element.40.refs_1_, bf16[256,768]{1,0:T(8,128)(2,1)S(1)} %get-tuple-element.41.refs_2_, bf16[256,768]{1,0:T(8,128)(2,1)S(1)} %get-tuple-element.42.refs_3_, bf16[256,768]{1,0:T(8,128)(2,1)} %get-tuple-element.43.refs_4_, ...), custom_call_target="tpu_custom_call" | custom-call | flops 1 | bytes 1 | tf_op jit(solution)/shard_map/cond/branch_1_fun/table/pallas_call | solution.py:185
  360.7 3.0 collective-permute-start.58
  368.7 4.9 %collective-permute-done.36.refs_3_ = bf16[48,2688]{1,0:T(8,128)(2,1)S(1)} collective-permute-done((bf16[48,2688]{1,0:T(8,128)(2,1)S(1)}, bf16[48,2688]{1,0:T(8,128)(2,1)S(1)}, u32[]{:S(2)}, u32[]{:S(2)}) %collective-permute-start.36) | collective-permute-done | bytes 258080 | tf_op jit(solution)/shard_map/ppermute | solution.py:1442
  373.6 1.5 collective-permute-start.38
  375.8 3.2 features_assemble.1
  379.0 3.0 ff_assemble.1
  382.0 2.6 kv_assemble.1
  384.7 2.4 tail_assemble.1
  (335 shorter events, 84.1 us)
Async XLA Ops:
  0.7 57.2 %copy-start = (s32[16]{0:T(128)S(1)}, s32[16]{0:T(128)}, u32[]{:S(2)}) copy-start(s32[16]{0:T(128)} %param.35) | copy-start | bytes 196
  3.3 17.1 %collective-permute-start.5 = (bf16[8,32,1408]{2,1,0:T(8,128)(2,1)}, bf16[8,32,1408]{2,1,0:T(8,128)(2,1)}, u32[]{:S(2)}, u32[]{:S(2)}) collective-permute-start(bf16[8,32,1408]{2,1,0:T(8,128)(2,1)} %get-tuple-element.279), channel_id=1, source_target_pairs={{0,1},{1,0},{2,3},{3,2},{4,5},{5,4},{6,7},{7,6},{8,9},{9,8},{10,11... | collective-permute-start | bytes 2162696 | tf_op jit(solution)/shard_map/ppermute | solution.py:1438
  6.1 27.6 %copy-start.2 = (bf16[768,2304]{1,0:T(8,128)(2,1)S(1)}, bf16[768,2304]{1,0:T(8,128)(2,1)}, u32[]{:S(2)}) copy-start(bf16[768,2304]{1,0:T(8,128)(2,1)} %refs_14_.1) | copy-start | bytes 10616836
  14.5 2.1 collective-permute-start.3
  17.7 12.0 %collective-permute-start.4 = (bf16[256,768]{1,0:T(8,128)(2,1)S(1)}, bf16[256,768]{1,0:T(8,128)(2,1)S(1)}, u32[]{:S(2)}, u32[]{:S(2)}) collective-permute-start(bf16[256,768]{1,0:T(8,128)(2,1)S(1)} %add.91.refs_11_.refs_4_.refs_16_), channel_id=1, source_target_pairs={{0,2},{2,0},{1,3},{3,1},{4,6},{6,4},{5,7},{7,5},{8,10},{10,8},{9,1... | collective-permute-start | bytes 1179656 | tf_op jit(solution)/shard_map/ppermute | solution.py:1442
  23.8 27.4 %collective-permute-start.8 = (bf16[352,768]{1,0:T(8,128)(2,1)}, bf16[352,768]{1,0:T(8,128)(2,1)}, u32[]{:S(2)}, u32[]{:S(2)}) collective-permute-start(bf16[352,768]{1,0:T(8,128)(2,1)} %get-tuple-element.181), channel_id=1, source_target_pairs={{0,2},{2,0},{1,3},{3,1},{4,6},{6,4},{5,7},{7,5},{8,10},{10,8},{9,1... | collective-permute-start | bytes 1622024 | tf_op jit(solution)/shard_map/ppermute | solution.py:1442
  23.8 29.2 %collective-permute-start.9 = (bf16[352,768]{1,0:T(8,128)(2,1)}, bf16[352,768]{1,0:T(8,128)(2,1)}, u32[]{:S(2)}, u32[]{:S(2)}) collective-permute-start(bf16[352,768]{1,0:T(8,128)(2,1)} %get-tuple-element.182), channel_id=1, source_target_pairs={{0,2},{2,0},{1,3},{3,1},{4,6},{6,4},{5,7},{7,5},{8,10},{10,8},{9,1... | collective-permute-start | bytes 1622024 | tf_op jit(solution)/shard_map/ppermute | solution.py:1442
  25.3 32.4 %collective-permute-start.10 = (bf16[352,768]{1,0:T(8,128)(2,1)}, bf16[352,768]{1,0:T(8,128)(2,1)}, u32[]{:S(2)}, u32[]{:S(2)}) collective-permute-start(bf16[352,768]{1,0:T(8,128)(2,1)} %refs_4_.9), channel_id=1, source_target_pairs={{0,1},{1,0},{2,3},{3,2},{4,5},{5,4},{6,7},{7,6},{8,9},{9,8},{10,11... | collective-permute-start | bytes 1622024 | tf_op jit(solution)/shard_map/ppermute | solution.py:1438
  26.3 45.8 %collective-permute-start.6 = (bf16[8,32,1408]{2,1,0:T(8,128)(2,1)}, bf16[8,32,1408]{2,1,0:T(8,128)(2,1)}, u32[]{:S(2)}, u32[]{:S(2)}) collective-permute-start(bf16[8,32,1408]{2,1,0:T(8,128)(2,1)} %get-tuple-element.280.refs_2_.refs_3_), channel_id=1, source_target_pairs={{0,2},{2,0},{1,3},{3,1},{4,6},{6,4},{5,7},{7,5},{8,10},{10,8},{9,1... | collective-permute-start | bytes 2162696 | tf_op jit(solution)/shard_map/ppermute | solution.py:1442
  30.4 53.4 %collective-permute-start.7 = (bf16[8,32,1408]{2,1,0:T(8,128)(2,1)}, bf16[8,32,1408]{2,1,0:T(8,128)(2,1)}, u32[]{:S(2)}, u32[]{:S(2)}) collective-permute-start(bf16[8,32,1408]{2,1,0:T(8,128)(2,1)} %get-tuple-element.180), channel_id=1, source_target_pairs={{0,2},{2,0},{1,3},{3,1},{4,6},{6,4},{5,7},{7,5},{8,10},{10,8},{9,1... | collective-permute-start | bytes 2162696 | tf_op jit(solution)/shard_map/ppermute | solution.py:1442
  51.2 20.9 %collective-permute-start.12 = (bf16[352,768]{1,0:T(8,128)(2,1)}, bf16[352,768]{1,0:T(8,128)(2,1)}, u32[]{:S(2)}, u32[]{:S(2)}) collective-permute-start(bf16[352,768]{1,0:T(8,128)(2,1)} %refs_8_.13), channel_id=1, source_target_pairs={{0,1},{1,0},{2,3},{3,2},{4,5},{5,4},{6,7},{7,6},{8,9},{9,8},{10,11... | collective-permute-start | bytes 1622024 | tf_op jit(solution)/shard_map/ppermute | solution.py:1438
  56.7 27.1 %collective-permute-start.11 = (bf16[352,768]{1,0:T(8,128)(2,1)}, bf16[352,768]{1,0:T(8,128)(2,1)}, u32[]{:S(2)}, u32[]{:S(2)}) collective-permute-start(bf16[352,768]{1,0:T(8,128)(2,1)} %get-tuple-element.184.refs_7_.refs_5_), channel_id=1, source_target_pairs={{0,1},{1,0},{2,3},{3,2},{4,5},{5,4},{6,7},{7,6},{8,9},{9,8},{10,11... | collective-permute-start | bytes 1622024 | tf_op jit(solution)/shard_map/ppermute | solution.py:1438
  57.7 26.1 %collective-permute-start.13 = (bf16[352,768]{1,0:T(8,128)(2,1)}, bf16[352,768]{1,0:T(8,128)(2,1)}, u32[]{:S(2)}, u32[]{:S(2)}) collective-permute-start(bf16[352,768]{1,0:T(8,128)(2,1)} %get-tuple-element.185.refs_11_.refs_9_), channel_id=1, source_target_pairs={{0,1},{1,0},{2,3},{3,2},{4,5},{5,4},{6,7},{7,6},{8,9},{9,8},{10,11... | collective-permute-start | bytes 1622024 | tf_op jit(solution)/shard_map/ppermute | solution.py:1438
  59.8 24.0 %copy-start.78 = (s32[4]{0:T(128)}, s32[4]{0:T(128)S(1)}, u32[]{:S(2)}) copy-start(s32[4]{0:T(128)S(1)} %pad_add_fusion.refs_1_) | copy-start | bytes 52
  60.6 51.3 %copy-start.101 = (f32[8,33]{1,0:T(8,128)}, f32[8,33]{1,0:T(8,128)S(1)}, u32[]{:S(2)}) copy-start(f32[8,33]{1,0:T(8,128)S(1)} %add_convert_fusion.7) | copy-start | bytes 3172
  113.2 1.9 collective-permute-start.16
  113.9 7.0 %collective-permute-start.15 = (bf16[256,768]{1,0:T(8,128)(2,1)}, bf16[256,768]{1,0:T(8,128)(2,1)}, u32[]{:S(2)}, u32[]{:S(2)}) collective-permute-start(bf16[256,768]{1,0:T(8,128)(2,1)} %get-tuple-element.193.refs_2_.refs_9_), channel_id=1, source_target_pairs={{0,1},{1,0},{2,3},{3,2},{4,5},{5,4},{6,7},{7,6},{8,9},{9,8},{10,11... | collective-permute-start | bytes 1179656 | tf_op jit(solution)/shard_map/ppermute | solution.py:1438
  113.9 43.8 %collective-permute-start.21 = (bf16[960,256]{1,0:T(8,128)(2,1)}, bf16[960,256]{1,0:T(8,128)(2,1)}, u32[]{:S(2)}, u32[]{:S(2)}) collective-permute-start(bf16[960,256]{1,0:T(8,128)(2,1)} %get-tuple-element.205), channel_id=1, source_target_pairs={{0,1},{1,0},{2,3},{3,2},{4,5},{5,4},{6,7},{7,6},{8,9},{9,8},{10,11... | collective-permute-start | bytes 1474568 | tf_op jit(solution)/shard_map/ppermute | solution.py:1438
  114.4 20.1 %collective-permute-start.14 = (bf16[256,768]{1,0:T(8,128)(2,1)}, bf16[256,768]{1,0:T(8,128)(2,1)}, u32[]{:S(2)}, u32[]{:S(2)}) collective-permute-start(bf16[256,768]{1,0:T(8,128)(2,1)} %get-tuple-element.192.refs_1_.refs_7_), channel_id=1, source_target_pairs={{0,1},{1,0},{2,3},{3,2},{4,5},{5,4},{6,7},{7,6},{8,9},{9,8},{10,11... | collective-permute-start | bytes 1179656 | tf_op jit(solution)/shard_map/ppermute | solution.py:1438
  114.4 43.3 %collective-permute-start.22 = (bf16[960,256]{1,0:T(8,128)(2,1)}, bf16[960,256]{1,0:T(8,128)(2,1)}, u32[]{:S(2)}, u32[]{:S(2)}) collective-permute-start(bf16[960,256]{1,0:T(8,128)(2,1)} %get-tuple-element.210), channel_id=1, source_target_pairs={{0,1},{1,0},{2,3},{3,2},{4,5},{5,4},{6,7},{7,6},{8,9},{9,8},{10,11... | collective-permute-start | bytes 1474568 | tf_op jit(solution)/shard_map/ppermute | solution.py:1438
  115.9 2.9 collective-permute-start.17
  118.8 38.9 %collective-permute-start.23 = (bf16[192,1024]{1,0:T(8,128)(2,1)}, bf16[192,1024]{1,0:T(8,128)(2,1)}, u32[]{:S(2)}, u32[]{:S(2)}) collective-permute-start(bf16[192,1024]{1,0:T(8,128)(2,1)} %copy-done.88), channel_id=1, source_target_pairs={{0,1},{1,0},{2,3},{3,2},{4,5},{5,4},{6,7},{7,6},{8,9},{9,8},{10,11... | collective-permute-start | bytes 1179656 | tf_op jit(solution)/shard_map/ppermute | solution.py:1438
  120.9 4.4 %collective-permute-start.18 = (f32[32,640]{1,0:T(8,128)}, f32[32,640]{1,0:T(8,128)S(1)}, u32[]{:S(2)}, u32[]{:S(2)}) collective-permute-start(f32[32,640]{1,0:T(8,128)} %pad_maximum_fusion.4.refs_2_), channel_id=1, source_target_pairs={{0,8},{8,0},{16,24},{24,16},{1,9},{9,1},{17,25},{25,17},{2,10},{10... | collective-permute-start | bytes 245768 | tf_op jit(solution)/shard_map/ppermute | solution.py:1450
  126.0 4.4 %collective-permute-start.19 = (f32[32,640]{1,0:T(8,128)}, f32[32,640]{1,0:T(8,128)S(1)}, u32[]{:S(2)}, u32[]{:S(2)}) collective-permute-start(f32[32,640]{1,0:T(8,128)} %pad_maximum_fusion.4.refs_2_), channel_id=1, source_target_pairs={{0,16},{8,24},{16,0},{24,8},{1,17},{9,25},{17,1},{25,9},{2,18},{10... | collective-permute-start | bytes 245768 | tf_op jit(solution)/shard_map/ppermute | solution.py:1450
  131.1 26.6 %collective-permute-start.24 = (bf16[192,256]{1,0:T(8,128)(2,1)}, bf16[192,256]{1,0:T(8,128)(2,1)}, u32[]{:S(2)}, u32[]{:S(2)}) collective-permute-start(bf16[192,256]{1,0:T(8,128)(2,1)} %copy-done.91), channel_id=1, source_target_pairs={{0,1},{1,0},{2,3},{3,2},{4,5},{5,4},{6,7},{7,6},{8,9},{9,8},{10,11... | collective-permute-start | bytes 294920 | tf_op jit(solution)/shard_map/ppermute | solution.py:1438
  134.6 6.4 %collective-permute-start.20 = (f32[32,640]{1,0:T(8,128)}, f32[32,640]{1,0:T(8,128)}, u32[]{:S(2)}, u32[]{:S(2)}) collective-permute-start(f32[32,640]{1,0:T(8,128)} %pad_maximum_fusion.4.refs_2_), channel_id=1, source_target_pairs={{0,24},{8,16},{16,8},{24,0},{1,25},{9,17},{17,9},{25,1},{2,26},{10... | collective-permute-start | bytes 245768 | tf_op jit(solution)/shard_map/ppermute | solution.py:1450
  157.1 19.1 %collective-permute-start.26 = (bf16[256,3840]{1,0:T(8,128)(2,1)}, bf16[256,3840]{1,0:T(8,128)(2,1)}, u32[]{:S(2)}, u32[]{:S(2)}) collective-permute-start(bf16[256,3840]{1,0:T(8,128)(2,1)} %get-tuple-element.215.refs_3_), channel_id=1, source_target_pairs={{0,1},{1,0},{2,3},{3,2},{4,5},{5,4},{6,7},{7,6},{8,9},{9,8},{10,11... | collective-permute-start | bytes 5898248 | tf_op jit(solution)/shard_map/ppermute | solution.py:1438
  176.1 6.6 %collective-permute-start.25 = (bf16[256,3840]{1,0:T(8,128)(2,1)}, bf16[256,3840]{1,0:T(8,128)(2,1)S(1)}, u32[]{:S(2)}, u32[]{:S(2)}) collective-permute-start(bf16[256,3840]{1,0:T(8,128)(2,1)} %get-tuple-element.213.refs_3_), channel_id=1, source_target_pairs={{0,1},{1,0},{2,3},{3,2},{4,5},{5,4},{6,7},{7,6},{8,9},{9,8},{10,11... | collective-permute-start | bytes 5898248 | tf_op jit(solution)/shard_map/ppermute | solution.py:1438
  187.6 33.7 %collective-permute-start.28 = (bf16[4,192,768]{2,1,0:T(8,128)(2,1)}, bf16[4,192,768]{2,1,0:T(8,128)(2,1)}, u32[]{:S(2)}, u32[]{:S(2)}) collective-permute-start(bf16[4,192,768]{2,1,0:T(8,128)(2,1)} %get-tuple-element.230), channel_id=1, source_target_pairs={{0,4},{4,0},{1,5},{5,1},{2,6},{6,2},{3,7},{7,3},{8,12},{12,8},{9,1... | collective-permute-start | bytes 3538952 | tf_op jit(solution)/shard_map/ppermute | solution.py:1450
  188.9 34.1 %collective-permute-start.27 = (bf16[4,192,768]{2,1,0:T(8,128)(2,1)}, bf16[4,192,768]{2,1,0:T(8,128)(2,1)}, u32[]{:S(2)}, u32[]{:S(2)}) collective-permute-start(bf16[4,192,768]{2,1,0:T(8,128)(2,1)} %get-tuple-element.229), channel_id=1, source_target_pairs={{0,8},{8,0},{16,24},{24,16},{1,9},{9,1},{17,25},{25,17},{2,10},{10... | collective-permute-start | bytes 3538952 | tf_op jit(solution)/shard_map/ppermute | solution.py:1450
  225.1 6.1 %collective-permute-start.29 = (bf16[256,768]{1,0:T(8,128)(2,1)S(1)}, bf16[256,768]{1,0:T(8,128)(2,1)S(1)}, u32[]{:S(2)}, u32[]{:S(2)}) collective-permute-start(bf16[256,768]{1,0:T(8,128)(2,1)S(1)} %stage.5.refs_2_), channel_id=1, source_target_pairs={{0,1},{1,0},{2,3},{3,2},{4,5},{5,4},{6,7},{7,6},{8,9},{9,8},{10,11... | collective-permute-start | bytes 1179656 | tf_op jit(solution)/shard_map/ppermute | solution.py:1438
  240.1 21.1 %collective-permute-start.46 = (bf16[8,176,384]{2,1,0:T(8,128)(2,1)S(1)}, bf16[8,176,384]{2,1,0:T(8,128)(2,1)S(1)}, u32[]{:S(2)}, u32[]{:S(2)}) collective-permute-start(bf16[8,176,384]{2,1,0:T(8,128)(2,1)S(1)} %get-tuple-element.256), channel_id=1, source_target_pairs={{0,1},{1,0},{2,3},{3,2},{4,5},{5,4},{6,7},{7,6},{8,9},{9,8},{10,11... | collective-permute-start | bytes 3244040 | tf_op jit(solution)/shard_map/ppermute | solution.py:1438
  240.2 6.1 %collective-permute-start.39 = (bf16[128,768]{1,0:T(8,128)(2,1)S(1)}, bf16[128,768]{1,0:T(8,128)(2,1)S(1)}, u32[]{:S(2)}, u32[]{:S(2)}) collective-permute-start(bf16[128,768]{1,0:T(8,128)(2,1)S(1)} %collect.1.refs_7_), channel_id=1, source_target_pairs={{0,4},{4,0},{1,5},{5,1},{2,6},{6,2},{3,7},{7,3},{8,12},{12,8},{9,1... | collective-permute-start | bytes 589832 | tf_op jit(solution)/shard_map/ppermute | solution.py:1450
  240.4 22.0 %collective-permute-start.32 = (bf16[256,1536]{1,0:T(8,128)(2,1)S(1)}, bf16[256,1536]{1,0:T(8,128)(2,1)S(1)}, u32[]{:S(2)}, u32[]{:S(2)}) collective-permute-start(bf16[256,1536]{1,0:T(8,128)(2,1)S(1)} %get-tuple-element.241.refs_5_), channel_id=1, source_target_pairs={{0,1},{1,0},{2,3},{3,2},{4,5},{5,4},{6,7},{7,6},{8,9},{9,8},{10,11... | collective-permute-start | bytes 2359304 | tf_op jit(solution)/shard_map/ppermute | solution.py:1438
  246.3 10.8 %collective-permute-start.40 = (bf16[256,768]{1,0:T(8,128)(2,1)S(1)}, bf16[256,768]{1,0:T(8,128)(2,1)S(1)}, u32[]{:S(2)}, u32[]{:S(2)}) collective-permute-start(bf16[256,768]{1,0:T(8,128)(2,1)S(1)} %pad_maximum_fusion.2), channel_id=1, source_target_pairs={{0,8},{8,16},{16,24},{1,9},{9,17},{17,25},{2,10},{10,18},{18,26},{... | collective-permute-start | bytes 1179656 | tf_op jit(solution)/shard_map/ppermute | solution.py:1479
  250.0 15.9 %collective-permute-start.31 = (bf16[304,3840]{1,0:T(8,128)(2,1)S(1)}, bf16[304,3840]{1,0:T(8,128)(2,1)S(1)}, u32[]{:S(2)}, u32[]{:S(2)}) collective-permute-start(bf16[304,3840]{1,0:T(8,128)(2,1)S(1)} %get-tuple-element.239.refs_4_), channel_id=1, source_target_pairs={{0,1},{1,0},{2,3},{3,2},{4,5},{5,4},{6,7},{7,6},{8,9},{9,8},{10,11... | collective-permute-start | bytes 7004168 | tf_op jit(solution)/shard_map/ppermute | solution.py:1438
  251.6 21.7 %collective-permute-start.55 = (bf16[2,192,768]{2,1,0:T(8,128)(2,1)S(1)}, bf16[2,192,768]{2,1,0:T(8,128)(2,1)S(1)}, u32[]{:S(2)}, u32[]{:S(2)}) collective-permute-start(bf16[2,192,768]{2,1,0:T(8,128)(2,1)S(1)} %get-tuple-element.231.refs_3_), channel_id=1, source_target_pairs={{0,8},{8,0},{16,24},{24,16},{1,9},{9,1},{17,25},{25,17},{2,10},{10... | collective-permute-start | bytes 1769480 | tf_op jit(solution)/shard_map/ppermute | solution.py:1450
  257.1 30.3 %copy-start.93 = (bf16[256,768]{1,0:T(8,128)(2,1)}, bf16[256,768]{1,0:T(8,128)(2,1)S(1)}, u32[]{:S(2)}) copy-start(bf16[256,768]{1,0:T(8,128)(2,1)S(1)} %collective-permute-done.40.refs_3_) | copy-start | bytes 1179652
  257.1 27.9 %collective-permute-start.53 = (bf16[2,192,768]{2,1,0:T(8,128)(2,1)S(1)}, bf16[2,192,768]{2,1,0:T(8,128)(2,1)S(1)}, u32[]{:S(2)}, u32[]{:S(2)}) collective-permute-start(bf16[2,192,768]{2,1,0:T(8,128)(2,1)S(1)} %get-tuple-element.232.refs_2_.refs_4_), channel_id=1, source_target_pairs={{0,16},{8,24},{16,0},{24,8},{1,17},{9,25},{17,1},{25,9},{2,18},{10... | collective-permute-start | bytes 1769480 | tf_op jit(solution)/shard_map/ppermute | solution.py:1450
  262.1 23.9 %collective-permute-start.47 = (bf16[4,176,384]{2,1,0:T(8,128)(2,1)S(1)}, bf16[4,176,384]{2,1,0:T(8,128)(2,1)S(1)}, u32[]{:S(2)}, u32[]{:S(2)}) collective-permute-start(bf16[4,176,384]{2,1,0:T(8,128)(2,1)S(1)} %get-tuple-element.281), channel_id=1, source_target_pairs={{0,4},{4,0},{1,5},{5,1},{2,6},{6,2},{3,7},{7,3},{8,12},{12,8},{9,1... | collective-permute-start | bytes 1622024 | tf_op jit(solution)/shard_map/ppermute | solution.py:1450
  268.3 41.3 %collective-permute-start.33 = (bf16[4,48,2688]{2,1,0:T(8,128)(2,1)S(1)}, bf16[4,48,2688]{2,1,0:T(8,128)(2,1)S(1)}, u32[]{:S(2)}, u32[]{:S(2)}) collective-permute-start(bf16[4,48,2688]{2,1,0:T(8,128)(2,1)S(1)} %get-tuple-element.243), channel_id=1, source_target_pairs={{0,4},{4,0},{1,5},{5,1},{2,6},{6,2},{3,7},{7,3},{8,12},{12,8},{9,1... | collective-permute-start | bytes 3096584 | tf_op jit(solution)/shard_map/ppermute | solution.py:1450
  268.8 18.5 %collective-permute-start.43 = (bf16[256,768]{1,0:T(8,128)(2,1)S(1)}, bf16[256,768]{1,0:T(8,128)(2,1)S(1)}, u32[]{:S(2)}, u32[]{:S(2)}) collective-permute-start(bf16[256,768]{1,0:T(8,128)(2,1)S(1)} %pad_maximum_fusion.2), channel_id=1, source_target_pairs={{8,0},{16,8},{24,16},{9,1},{17,9},{25,17},{10,2},{18,10},{26,18},{... | collective-permute-start | bytes 1179656 | tf_op jit(solution)/shard_map/ppermute | solution.py:1480
  273.9 32.1 %collective-permute-start.56 = (bf16[1,192,768]{2,1,0:T(8,128)(2,1)S(1)}, bf16[1,192,768]{2,1,0:T(8,128)(2,1)S(1)}, u32[]{:S(2)}, u32[]{:S(2)}) collective-permute-start(bf16[1,192,768]{2,1,0:T(8,128)(2,1)S(1)} %get-tuple-element.269), channel_id=1, source_target_pairs={{0,16},{8,24},{16,0},{24,8},{1,17},{9,25},{17,1},{25,9},{2,18},{10... | collective-permute-start | bytes 884744 | tf_op jit(solution)/shard_map/ppermute | solution.py:1450
  285.6 22.5 %collective-permute-start.54 = (bf16[1,192,768]{2,1,0:T(8,128)(2,1)S(1)}, bf16[1,192,768]{2,1,0:T(8,128)(2,1)S(1)}, u32[]{:S(2)}, u32[]{:S(2)}) collective-permute-start(bf16[1,192,768]{2,1,0:T(8,128)(2,1)S(1)} %get-tuple-element.266), channel_id=1, source_target_pairs={{0,4},{4,0},{1,5},{5,1},{2,6},{6,2},{3,7},{7,3},{8,12},{12,8},{9,1... | collective-permute-start | bytes 884744 | tf_op jit(solution)/shard_map/ppermute | solution.py:1450
  286.6 20.8 %collective-permute-start.48 = (bf16[2,176,384]{2,1,0:T(8,128)(2,1)S(1)}, bf16[2,176,384]{2,1,0:T(8,128)(2,1)S(1)}, u32[]{:S(2)}, u32[]{:S(2)}) collective-permute-start(bf16[2,176,384]{2,1,0:T(8,128)(2,1)S(1)} %get-tuple-element.258), channel_id=1, source_target_pairs={{0,8},{8,0},{16,24},{24,16},{1,9},{9,1},{17,25},{25,17},{2,10},{10... | collective-permute-start | bytes 811016 | tf_op jit(solution)/shard_map/ppermute | solution.py:1450
  287.3 30.3 %collective-permute-start.41 = (bf16[256,768]{1,0:T(8,128)(2,1)S(1)}, bf16[256,768]{1,0:T(8,128)(2,1)}, u32[]{:S(2)}, u32[]{:S(2)}) collective-permute-start(bf16[256,768]{1,0:T(8,128)(2,1)S(1)} %collective-permute-done.40.refs_3_), channel_id=1, source_target_pairs={{0,8},{8,16},{16,24},{1,9},{9,17},{17,25},{2,10},{10,18},{18,26},{... | collective-permute-start | bytes 1179656 | tf_op jit(solution)/shard_map/ppermute | solution.py:1479
  306.0 14.1 %collective-permute-start.44 = (bf16[256,768]{1,0:T(8,128)(2,1)S(1)}, bf16[256,768]{1,0:T(8,128)(2,1)}, u32[]{:S(2)}, u32[]{:S(2)}) collective-permute-start(bf16[256,768]{1,0:T(8,128)(2,1)S(1)} %collective-permute-done.43), channel_id=1, source_target_pairs={{8,0},{16,8},{24,16},{9,1},{17,9},{25,17},{10,2},{18,10},{26,18},{... | collective-permute-start | bytes 1179656 | tf_op jit(solution)/shard_map/ppermute | solution.py:1480
  308.0 9.4 %collective-permute-start.49 = (bf16[1,176,384]{2,1,0:T(8,128)(2,1)S(1)}, bf16[1,176,384]{2,1,0:T(8,128)(2,1)S(1)}, u32[]{:S(2)}, u32[]{:S(2)}) collective-permute-start(bf16[1,176,384]{2,1,0:T(8,128)(2,1)S(1)} %get-tuple-element.260), channel_id=1, source_target_pairs={{0,16},{8,24},{16,0},{24,8},{1,17},{9,25},{17,1},{25,9},{2,18},{10... | collective-permute-start | bytes 405512 | tf_op jit(solution)/shard_map/ppermute | solution.py:1450
  308.2 25.4 %copy-start.79 = (s32[4]{0:T(128)S(1)}, s32[4]{0:T(128)}, u32[]{:S(2)}) copy-start(s32[4]{0:T(128)} %copy-done.78) | copy-start | bytes 52
  308.3 55.5 %collective-permute-start.57 = (bf16[384,768]{1,0:T(8,128)(2,1)S(1)}, bf16[384,768]{1,0:T(8,128)(2,1)S(1)}, u32[]{:S(2)}, u32[]{:S(2)}) collective-permute-start(bf16[384,768]{1,0:T(8,128)(2,1)S(1)} %pad_maximum_fusion.refs_2_), channel_id=1, source_target_pairs={{0,2},{2,0},{1,3},{3,1},{4,6},{6,4},{5,7},{7,5},{8,10},{10,8},{9,1... | collective-permute-start | bytes 1769480 | tf_op jit(solution)/shard_map/ppermute | solution.py:1442
  310.3 21.9 %collective-permute-start.34 = (bf16[2,48,2688]{2,1,0:T(8,128)(2,1)S(1)}, bf16[2,48,2688]{2,1,0:T(8,128)(2,1)S(1)}, u32[]{:S(2)}, u32[]{:S(2)}) collective-permute-start(bf16[2,48,2688]{2,1,0:T(8,128)(2,1)S(1)} %get-tuple-element.245), channel_id=1, source_target_pairs={{0,8},{8,0},{16,24},{24,16},{1,9},{9,1},{17,25},{25,17},{2,10},{10... | collective-permute-start | bytes 1548296 | tf_op jit(solution)/shard_map/ppermute | solution.py:1450
  317.5 9.5 %collective-permute-start.50 = (bf16[1,176,384]{2,1,0:T(8,128)(2,1)S(1)}, bf16[1,176,384]{2,1,0:T(8,128)(2,1)S(1)}, u32[]{:S(2)}, u32[]{:S(2)}) collective-permute-start(bf16[1,176,384]{2,1,0:T(8,128)(2,1)S(1)} %add_convert_fusion.6), channel_id=1, source_target_pairs={{0,16},{8,24},{16,0},{24,8},{1,17},{9,25},{17,1},{25,9},{2,18},{10... | collective-permute-start | bytes 405512 | tf_op jit(solution)/shard_map/ppermute | solution.py:1450
  317.6 23.2 %collective-permute-start.42 = (bf16[256,768]{1,0:T(8,128)(2,1)}, bf16[256,768]{1,0:T(8,128)(2,1)}, u32[]{:S(2)}, u32[]{:S(2)}) collective-permute-start(bf16[256,768]{1,0:T(8,128)(2,1)} %collective-permute-done.41), channel_id=1, source_target_pairs={{0,8},{8,16},{16,24},{1,9},{9,17},{17,25},{2,10},{10,18},{18,26},{... | collective-permute-start | bytes 1179656 | tf_op jit(solution)/shard_map/ppermute | solution.py:1479
  320.2 30.0 %collective-permute-start.45 = (bf16[256,768]{1,0:T(8,128)(2,1)}, bf16[256,768]{1,0:T(8,128)(2,1)}, u32[]{:S(2)}, u32[]{:S(2)}) collective-permute-start(bf16[256,768]{1,0:T(8,128)(2,1)} %collective-permute-done.44), channel_id=1, source_target_pairs={{8,0},{16,8},{24,16},{9,1},{17,9},{25,17},{10,2},{18,10},{26,18},{... | collective-permute-start | bytes 1179656 | tf_op jit(solution)/shard_map/ppermute | solution.py:1480
  327.8 36.1 %collective-permute-start.51 = (bf16[2,176,384]{2,1,0:T(8,128)(2,1)}, bf16[2,176,384]{2,1,0:T(8,128)(2,1)}, u32[]{:S(2)}, u32[]{:S(2)}) collective-permute-start(bf16[2,176,384]{2,1,0:T(8,128)(2,1)} %pad_maximum_fusion.3), channel_id=1, source_target_pairs={{0,8},{8,0},{16,24},{24,16},{1,9},{9,1},{17,25},{25,17},{2,10},{10... | collective-permute-start | bytes 811016 | tf_op jit(solution)/shard_map/ppermute | solution.py:1450
  332.9 32.5 %collective-permute-start.35 = (bf16[1,48,2688]{2,1,0:T(8,128)(2,1)S(1)}, bf16[1,48,2688]{2,1,0:T(8,128)(2,1)}, u32[]{:S(2)}, u32[]{:S(2)}) collective-permute-start(bf16[1,48,2688]{2,1,0:T(8,128)(2,1)S(1)} %get-tuple-element.247), channel_id=1, source_target_pairs={{0,16},{8,24},{16,0},{24,8},{1,17},{9,25},{17,1},{25,9},{2,18},{10... | collective-permute-start | bytes 774152 | tf_op jit(solution)/shard_map/ppermute | solution.py:1450
  340.8 26.9 %collective-permute-start.30 = (bf16[8,32,1408]{2,1,0:T(8,128)(2,1)}, bf16[8,32,1408]{2,1,0:T(8,128)(2,1)}, u32[]{:S(2)}, u32[]{:S(2)}) collective-permute-start(bf16[8,32,1408]{2,1,0:T(8,128)(2,1)} %get-tuple-element.236), channel_id=1, source_target_pairs={{0,1},{1,0},{2,3},{3,2},{4,5},{5,4},{6,7},{7,6},{8,9},{9,8},{10,11... | collective-permute-start | bytes 2162696 | tf_op jit(solution)/shard_map/ppermute | solution.py:1438
  350.2 24.9 %copy-start.84 = (f32[16,1]{1,0:T(8,128)S(1)}, f32[16,1]{1,0:T(8,128)}, u32[]{:S(2)}) copy-start(f32[16,1]{1,0:T(8,128)} %copy-done.83) | copy-start | bytes 196
  360.7 18.3 %collective-permute-start.58 = (bf16[384,768]{1,0:T(8,128)(2,1)S(1)}, bf16[384,768]{1,0:T(8,128)(2,1)S(1)}, u32[]{:S(2)}, u32[]{:S(2)}) collective-permute-start(bf16[384,768]{1,0:T(8,128)(2,1)S(1)} %pad_maximum_fusion.refs_2_), channel_id=1, source_target_pairs={{0,1},{1,0},{2,3},{3,2},{4,5},{5,4},{6,7},{7,6},{8,9},{9,8},{10,11... | collective-permute-start | bytes 1769480 | tf_op jit(solution)/shard_map/ppermute | solution.py:1438
  363.8 15.2 %collective-permute-start.59 = (bf16[384,768]{1,0:T(8,128)(2,1)S(1)}, bf16[384,768]{1,0:T(8,128)(2,1)S(1)}, u32[]{:S(2)}, u32[]{:S(2)}) collective-permute-start(bf16[384,768]{1,0:T(8,128)(2,1)S(1)} %collective-permute-done.57.refs_3_), channel_id=1, source_target_pairs={{0,1},{1,0},{2,3},{3,2},{4,5},{5,4},{6,7},{7,6},{8,9},{9,8},{10,11... | collective-permute-start | bytes 1769480 | tf_op jit(solution)/shard_map/ppermute | solution.py:1438
  365.0 17.0 %collective-permute-start.52 = (bf16[4,176,384]{2,1,0:T(8,128)(2,1)S(1)}, bf16[4,176,384]{2,1,0:T(8,128)(2,1)}, u32[]{:S(2)}, u32[]{:S(2)}) collective-permute-start(bf16[4,176,384]{2,1,0:T(8,128)(2,1)S(1)} %pad_maximum_fusion.1.refs_1_), channel_id=1, source_target_pairs={{0,4},{4,0},{1,5},{5,1},{2,6},{6,2},{3,7},{7,3},{8,12},{12,8},{9,1... | collective-permute-start | bytes 1622024 | tf_op jit(solution)/shard_map/ppermute | solution.py:1450
  366.4 7.2 %collective-permute-start.36 = (bf16[48,2688]{1,0:T(8,128)(2,1)S(1)}, bf16[48,2688]{1,0:T(8,128)(2,1)S(1)}, u32[]{:S(2)}, u32[]{:S(2)}) collective-permute-start(bf16[48,2688]{1,0:T(8,128)(2,1)S(1)} %fusion.14.refs_2_), channel_id=1, source_target_pairs={{0,2},{2,0},{1,3},{3,1},{4,6},{6,4},{5,7},{7,5},{8,10},{10,8},{9,1... | collective-permute-start | bytes 774152 | tf_op jit(solution)/shard_map/ppermute | solution.py:1442
  367.7 16.9 %collective-permute-start.37 = (bf16[48,2688]{1,0:T(8,128)(2,1)S(1)}, bf16[48,2688]{1,0:T(8,128)(2,1)}, u32[]{:S(2)}, u32[]{:S(2)}) collective-permute-start(bf16[48,2688]{1,0:T(8,128)(2,1)S(1)} %fusion.14.refs_2_), channel_id=1, source_target_pairs={{0,1},{1,0},{2,3},{3,2},{4,5},{5,4},{6,7},{7,6},{8,9},{9,8},{10,11... | collective-permute-start | bytes 774152 | tf_op jit(solution)/shard_map/ppermute | solution.py:1438
  373.6 11.0 %collective-permute-start.38 = (bf16[48,2688]{1,0:T(8,128)(2,1)S(1)}, bf16[48,2688]{1,0:T(8,128)(2,1)}, u32[]{:S(2)}, u32[]{:S(2)}) collective-permute-start(bf16[48,2688]{1,0:T(8,128)(2,1)S(1)} %collective-permute-done.36.refs_3_), channel_id=1, source_target_pairs={{0,1},{1,0},{2,3},{3,2},{4,5},{5,4},{6,7},{7,6},{8,9},{9,8},{10,11... | collective-permute-start | bytes 774152 | tf_op jit(solution)/shard_map/ppermute | solution.py:1438
  (102 other events, 542.9 us)
